TPU v7x, 32 devices: a whole 2x2x4 slice. The times are simulated.
32 devices in a mesh: rep: 1, fsdp: 32 (over z, y, x, core).
Axes of the slice: x: 2, y: 2, z: 4, core: 2. Of those that a mesh axis runs over, the one named last changes fastest.
Arguments:
- acts: bfloat16 [1, 8192, 2048], P('rep', 'fsdp'), may hold values from -6 to 6
- grad_out: bfloat16 [1, 8192, 1024], P('rep', 'fsdp'), may hold values from -0.13258252 to 0.13258252
- inner_weight: float32 [1, 2048, 1024], P('rep', 'fsdp'), may hold values from -0.03 to 0.03
- first_moment: float32 [1, 2048, 1024], P('rep', 'fsdp'), may hold values from -6 to 6
- second_moment: float32 [1, 2048, 1024], P('rep', 'fsdp'), may hold values from 0.1 to 10
- outer_weight: float32 [2048, 1024], P(('fsdp', 'rep')), may hold values from -0.03 to 0.03
- outer_momentum: float32 [2048, 1024], P(('fsdp', 'rep')), may hold values from -0.0006 to 0.0006
Outputs:
- outer_next: float32 [2048, 1024], P(('fsdp', 'rep'))
- momentum_next: float32 [2048, 1024], P(('fsdp', 'rep'))
- weight_next: bfloat16 [2048, 1024], P('fsdp')
All inputs are finite; a program needn't handle non-finite values.
Results may differ from a plain program's by a relative error of at most 0.008.
Values may be sent and summed in bfloat16 or wider, within the bound.
A program may use at most 64 MiB of HBM per device.

v0:
```python
import jax
import jax.numpy as jnp
from jax import lax
from jax.sharding import PartitionSpec as P

INNER_STEP = 500


def shards(acts, grad_out, inner_weight, first_moment, second_moment, outer_weight, outer_momentum):
    tokens = acts[0]
    cotangent = grad_out[0]
    grad = lax.psum_scatter(
        lax.dot_general(
            tokens, cotangent, (((0,), (0,)), ((), ())), preferred_element_type=jnp.float32
        ).astype(jnp.bfloat16),
        "fsdp",
        scatter_dimension=0,
        tiled=True,
    ).astype(jnp.float32)
    first = 0.9 * first_moment[0] + 0.1 * grad
    second = 0.95 * second_moment[0] + 0.05 * grad * grad
    first_hat = first / (1.0 - 0.9**INNER_STEP)
    second_hat = second / (1.0 - 0.95**INNER_STEP)
    inner_new = inner_weight[0] * (1.0 - 0.0004 * 0.1) - 0.0004 * first_hat / (
        jnp.sqrt(second_hat) + 1e-08
    )
    replicas = lax.axis_size("rep")
    summed = lax.psum_scatter(inner_new, "rep", scatter_dimension=0, tiled=True)
    pseudo = outer_weight - summed / replicas
    momentum_next = 0.9 * outer_momentum + pseudo
    outer_next = outer_weight - 0.7 * (pseudo + 0.9 * momentum_next)
    weight_next = lax.all_gather(outer_next.astype(jnp.bfloat16), "rep", axis=0, tiled=True)
    return (outer_next, momentum_next, weight_next)


def solution(mesh):
    placed = (
        P("rep", "fsdp", None),
        P("rep", "fsdp", None),
        P("rep", "fsdp", None),
        P("rep", "fsdp", None),
        P("rep", "fsdp", None),
        P(("fsdp", "rep"), None),
        P(("fsdp", "rep"), None),
    )
    return jax.shard_map(
        shards,
        mesh=mesh,
        in_specs=placed,
        out_specs=(P(("fsdp", "rep"), None), P(("fsdp", "rep"), None), P("fsdp", None)),
        check_vma=False,
    )
```

profile of v0, /device:TPU:0, one launch (start us, length us, event | category | flops | bytes accessed | tf_op | source)
XLA Modules:
  0.0 165.2 jit_solution(3320315842378671397)
XLA Ops:
  7.2 0.0 copy-start
  7.2 0.0 reduce-scatter.2.cloned.1.call-start
  7.2 1.2 copy-done
  8.4 4.3 %convolution_convert_fusion = bf16[2048,1024]{1,0:T(8,128)(2,1)} fusion(bf16[1,256,2048]{2,1,0:T(8,128)(2,1)S(1)} %copy-done, bf16[1,256,1024]{2,1,0:T(8,128)(2,1)} %param.8), kind=kOutput, calls=%fused_computation | convolution fusion | flops 1075838976 | bytes 5767168 | tf_op jit(solution)/shard_map/dot_general | solution.py:13
  12.7 0.0 copy-start.1
  12.7 0.0 copy-start.2
  12.7 0.0 copy-start.3
  12.7 0.0 copy-start.4
  12.7 0.0 copy-start.5
  12.7 0.0 reduce-scatter.2.cloned.1.call-update
  12.7 143.6 %reduce-scatter.2.cloned.1.call-done = bf16[64,1024]{1,0:T(8,128)(2,1)} async-done(((bf16[2048,1024]{1,0:T(8,128)(2,1)}), bf16[64,1024]{1,0:T(8,128)(2,1)}) %reduce-scatter.2.cloned.1.call-update) | async-done | bytes 131088 | tf_op jit(solution)/shard_map/reduce_scatter | solution.py:12
  156.3 0.0 copy-done.1
  156.3 0.0 copy-done.2
  156.3 0.0 copy-done.3
  156.3 0.0 copy-done.4
  156.3 0.0 copy-done.5
  156.4 2.0 %fusion.10 = (bf16[64,1024]{1,0:T(8,128)(2,1)}, f32[64,1024]{1,0:T(8,128)}, f32[64,1024]{1,0:T(8,128)}) fusion(f32[64,1024]{1,0:T(8,128)S(1)} %copy-done.1, f32[64,1024]{1,0:T(8,128)S(1)} %copy-done.2, f32[1,64,1024]{2,1,0:T(8,128)S(1)} %copy-done.3, bf16[64,1024]{1,0:T(8,128)(2,1)} %reduce-scatter.2.cloned.1.call-done, f32[1,64,1024]{2,1,0:T(8,128)S(1)} %copy-done.4, ...), kind=kLoop, calls=%fused_computation.15 | loop fusion | flops 1376256 | bytes 2097152 | tf_op jit(solution)/shard_map/convert_element_type | solution.py:32
Async XLA Ops:
  7.2 1.2 copy-start
  7.2 149.2 %reduce-scatter.2.cloned.1.call-start = ((), (), s32[]{:S(2)}) async-start(), calls=%async_computation.1 | async-start | bytes 4325376 | tf_op jit(solution)/shard_map/reduce_scatter | solution.py:12
  12.7 143.7 %copy-start.1 = (f32[64,1024]{1,0:T(8,128)S(1)}, f32[64,1024]{1,0:T(8,128)}, u32[]{:S(2)}) copy-start(f32[64,1024]{1,0:T(8,128)} %param.12) | copy-start | bytes 786436
  12.7 143.7 %copy-start.2 = (f32[64,1024]{1,0:T(8,128)S(1)}, f32[64,1024]{1,0:T(8,128)}, u32[]{:S(2)}) copy-start(f32[64,1024]{1,0:T(8,128)} %param.13) | copy-start | bytes 786436
  12.7 143.7 %copy-start.3 = (f32[1,64,1024]{2,1,0:T(8,128)S(1)}, f32[1,64,1024]{2,1,0:T(8,128)}, u32[]{:S(2)}) copy-start(f32[1,64,1024]{2,1,0:T(8,128)} %param.11) | copy-start | bytes 786436
  12.7 143.7 %copy-start.4 = (f32[1,64,1024]{2,1,0:T(8,128)S(1)}, f32[1,64,1024]{2,1,0:T(8,128)}, u32[]{:S(2)}) copy-start(f32[1,64,1024]{2,1,0:T(8,128)} %param.10) | copy-start | bytes 786436
  12.7 143.7 %copy-start.5 = (f32[1,64,1024]{2,1,0:T(8,128)S(1)}, f32[1,64,1024]{2,1,0:T(8,128)}, u32[]{:S(2)}) copy-start(f32[1,64,1024]{2,1,0:T(8,128)} %param.9) | copy-start | bytes 786436
Sparse Core Ops, SparseCore 0:
  12.8 143.4 reduce-scatter.1
where the time goes:
time: 165 us
  waiting for transfers between devices  144 us (87%)
  between operations  14.1 us (9%)
  matrix products  4.27 us (3%)
  other arithmetic  1.99 us (1%)
    reduce_scatter x1, waiting for transfers between devices, shards(): lax.psum_scatter(lax.dot_general(tokens, cotangent, (((0,), (0,)), ((), (...  144 us
    dot_general x1, matrix products, shards(): lax.dot_general(tokens, cotangent, (((0,), (0,)), ((), ())), preferred_el...  4.27 us
  transfers between devices with their start and end apart: 1, of which 1 were waited for; matrix products, arithmetic and copies ran while one was open for 0% of the time, Pallas kernels for 0%

commit v1 on v0

v1 whole, which is shorter than its diff:
```python
import functools

import jax
import jax.numpy as jnp
from jax import lax
from jax.experimental import pallas as pl
from jax.experimental.pallas import tpu as pltpu
from jax.sharding import PartitionSpec as P

INNER_STEP = 500
LANES = 128
WIDE = 2 * LANES
MESH = pl.DeviceIdType.MESH

ORDERS = (
    (1, 2, 3, 4),
    (2, 1, 3, 4),
    (3, 1, 2, 4),
    (3, 2, 1, 4),
    (1, 2, 3, 4),
    (2, 1, 3, 4),
    (1, 2, 3, 4),
    (2, 1, 3, 4),
)


def kernel(
    acts_hbm, cot_hbm, grad_ref,
    acts, cot, cot_peer, lhs, lhs_peer, part, in0, in1, in2, in3,
    load_sem, cot_send, cot_recv, lhs_send, lhs_recv, send_sem, recv_sem,
):
    me = lax.axis_index("fsdp")
    bit = [lax.rem(me // (1 << b), 2) for b in range(5)]
    peer = [me + (1 - 2 * bit[b]) * (1 << b) for b in range(5)]
    core = bit[0]
    tokens, width = cot.shape
    rows, tiles = grad_ref.shape[0], acts.shape[1] // LANES
    groups = 4
    group_rows = lhs.shape[1] // groups
    pieces, chunks = width // WIDE, width // LANES
    incoming = (in0, in1, in2, in3)

    load_acts = pltpu.make_async_copy(acts_hbm, acts, load_sem.at[0])
    load_acts.start()
    load_cot = pltpu.make_async_copy(cot_hbm, cot, load_sem.at[1])
    load_cot.start()
    barrier = pltpu.get_barrier_semaphore()
    for b in range(5):
        pl.semaphore_signal(barrier, inc=1, device_id={"fsdp": peer[b]}, device_id_type=MESH)

    def to_core(src, dst, send, recv):
        return pltpu.make_async_remote_copy(
            src_ref=src, dst_ref=dst, send_sem=send, recv_sem=recv,
            device_id={"fsdp": peer[0]}, device_id_type=MESH,
        )

    def cot_copy(j):
        cut = pl.ds(j * WIDE, WIDE)
        return to_core(cot_hbm.at[:, cut], cot_peer.at[:, cut], cot_send.at[j], cot_recv.at[j])

    def lhs_copy(g):
        cut = pl.ds(g * group_rows, group_rows)
        return to_core(lhs.at[1 - core, cut], lhs_peer.at[cut], lhs_send.at[g], lhs_recv.at[g])

    load_acts.wait()
    for t in range(tiles):
        turned = acts[:, t * LANES:(t + 1) * LANES].T
        lhs[0, t * rows:(t + 1) * rows, :] = turned[:rows]
        lhs[1, t * rows:(t + 1) * rows, :] = turned[rows:]
    pl.semaphore_wait(barrier, 5)
    cot_copy(0).start()
    for g in range(groups):
        lhs_copy(g).start()
    for j in range(1, pieces):
        cot_copy(j).start()

    def exchange(c, s):
        order = ORDERS[c % len(ORDERS)]
        kept = tuple(bit[b] for b in order[:s])
        return pltpu.make_async_remote_copy(
            src_ref=part.at[(c, *kept, 1 - bit[order[s]])],
            dst_ref=incoming[s].at[c],
            send_sem=send_sem.at[c, s],
            recv_sem=recv_sem.at[c, s],
            device_id={"fsdp": peer[order[s]]},
            device_id_type=MESH,
        )

    load_cot.wait()
    for j in range(pieces):
        cut = slice(j * WIDE, (j + 1) * WIDE)
        cot_copy(j).wait_recv()
        for g in range(groups):
            if j == 0:
                lhs_copy(g).wait_recv()
            block = slice(g * group_rows, (g + 1) * group_rows)
            product = jnp.dot(lhs[core, block, :], cot[:, cut], preferred_element_type=jnp.float32)
            product += jnp.dot(lhs_peer[block, :], cot_peer[:, cut], preferred_element_type=jnp.float32)
            product = product.astype(jnp.bfloat16)
            for k in range(group_rows // rows):
                t = g * (group_rows // rows) + k
                for h in range(2):
                    c = 2 * j + h
                    where = tuple((t >> (b - 1)) & 1 for b in ORDERS[c % len(ORDERS)])
                    part[(c, *where)] = product[k * rows:(k + 1) * rows, h * LANES:(h + 1) * LANES]
        exchange(2 * j, 0).start()
        exchange(2 * j + 1, 0).start()

    for s in range(4):
        for c in range(chunks):
            order = ORDERS[c % len(ORDERS)]
            exchange(c, s).wait_recv()
            kept = (c, *(bit[b] for b in order[: s + 1]))
            total = part[kept].astype(jnp.float32) + incoming[s][c].astype(jnp.float32)
            if s < 3:
                part[kept] = total.astype(jnp.bfloat16)
                exchange(c, s + 1).start()
            else:
                grad_ref[:, c * LANES:(c + 1) * LANES] = total
    for j in range(pieces):
        cot_copy(j).wait_send()
    for g in range(groups):
        lhs_copy(g).wait_send()
    for s in range(4):
        for c in range(chunks):
            exchange(c, s).wait_send()


def gradient(tokens, cotangent, devices):
    count, depth = tokens.shape
    width = cotangent.shape[1]
    rows, half, chunks = depth // devices, depth // 2, width // LANES
    bf16 = jnp.bfloat16
    return pl.pallas_call(
        kernel,
        out_shape=jax.ShapeDtypeStruct((rows, width), jnp.float32),
        in_specs=[pl.BlockSpec(memory_space=pl.ANY)] * 2,
        out_specs=pl.BlockSpec(memory_space=pltpu.VMEM),
        scratch_shapes=[
            pltpu.VMEM((count, depth), bf16),
            pltpu.VMEM((count, width), bf16),
            pltpu.VMEM((count, width), bf16),
            pltpu.VMEM((2, half, count), bf16),
            pltpu.VMEM((half, count), bf16),
            pltpu.VMEM((chunks, 2, 2, 2, 2, rows, LANES), bf16),
            pltpu.VMEM((chunks, 2, 2, 2, rows, LANES), bf16),
            pltpu.VMEM((chunks, 2, 2, rows, LANES), bf16),
            pltpu.VMEM((chunks, 2, rows, LANES), bf16),
            pltpu.VMEM((chunks, rows, LANES), bf16),
            pltpu.SemaphoreType.DMA((2,)),
            pltpu.SemaphoreType.DMA((width // WIDE,)),
            pltpu.SemaphoreType.DMA((width // WIDE,)),
            pltpu.SemaphoreType.DMA((4,)),
            pltpu.SemaphoreType.DMA((4,)),
            pltpu.SemaphoreType.DMA((chunks, 4)),
            pltpu.SemaphoreType.DMA((chunks, 4)),
        ],
        compiler_params=pltpu.CompilerParams(
            collective_id=0, has_side_effects=True, vmem_limit_bytes=48 * 1024 * 1024
        ),
        cost_estimate=pl.CostEstimate(
            flops=2 * count * depth * width,
            bytes_accessed=2 * count * (depth + width) + 4 * rows * width,
            transcendentals=0,
        ),
    )(tokens, cotangent)


def shards(devices, acts, grad_out, inner_weight, first_moment, second_moment, outer_weight, outer_momentum):
    grad = gradient(acts[0], grad_out[0], devices)
    first = 0.9 * first_moment[0] + 0.1 * grad
    second = 0.95 * second_moment[0] + 0.05 * grad * grad
    first_hat = first / (1.0 - 0.9**INNER_STEP)
    second_hat = second / (1.0 - 0.95**INNER_STEP)
    inner_new = inner_weight[0] * (1.0 - 0.0004 * 0.1) - 0.0004 * first_hat / (
        jnp.sqrt(second_hat) + 1e-08
    )
    replicas = lax.axis_size("rep")
    if replicas > 1:
        inner_new = lax.psum_scatter(inner_new, "rep", scatter_dimension=0, tiled=True) / replicas
    pseudo = outer_weight - inner_new
    momentum_next = 0.9 * outer_momentum + pseudo
    outer_next = outer_weight - 0.7 * (pseudo + 0.9 * momentum_next)
    weight_next = outer_next.astype(jnp.bfloat16)
    if replicas > 1:
        weight_next = lax.all_gather(weight_next, "rep", axis=0, tiled=True)
    return (outer_next, momentum_next, weight_next)


def solution(mesh):
    placed = (
        P("rep", "fsdp", None),
        P("rep", "fsdp", None),
        P("rep", "fsdp", None),
        P("rep", "fsdp", None),
        P("rep", "fsdp", None),
        P(("fsdp", "rep"), None),
        P(("fsdp", "rep"), None),
    )
    return jax.shard_map(
        functools.partial(shards, mesh.shape["fsdp"]),
        mesh=mesh,
        in_specs=placed,
        out_specs=(P(("fsdp", "rep"), None), P(("fsdp", "rep"), None), P("fsdp", None)),
        check_vma=False,
    )
```

time: 165 us -> 37.3 us (0.23)
  waiting for transfers between devices: 144 us -> 0 us
  Pallas kernels: 0 us -> 33 us
  between operations: 14.1 us -> 0.7 us
  matrix products: 4.27 us -> 0 us
    reduce_scatter x1 -> x0, waiting for transfers between devices: 144 us -> none  [shards(): lax.psum_scatter(lax.dot_general(tokens, cotangent, (((0,), (0,)), ((), (...]
    pallas_call x0 -> x1, Pallas kernels: none -> 33 us  [gradient(): pl.pallas_call(kernel, out_shape=jax.ShapeDtypeStruct((rows, width), jnp....]
    dot_general x1 -> x0, matrix products: 4.27 us -> none  [shards(): lax.dot_general(tokens, cotangent, (((0,), (0,)), ((), ())), preferred_el...]
  transfers between devices with their start and end apart: 1 -> 0, of which waited for: 1 -> 0; matrix products, arithmetic and copies ran while one was open for 0% -> 0% of each run, Pallas kernels for 0% -> 0%
where the time goes in v1:
time: 37.3 us; the launch traced here: 37.1 us
  Pallas kernels  33 us (88%)
  local copies, waits for them, and re-layouts  2.28 us (6%)
  other arithmetic  1.07 us (3%)
  between operations  0.7 us (2%)
    pallas_call x1, Pallas kernels, gradient(): pl.pallas_call(kernel, out_shape=jax.ShapeDtypeStruct((rows, width), jnp....  33 us
    unnamed x14, local copies, waits for them, and re-layouts  2.28 us
    convert_element_type x1, other arithmetic, shards(): weight_next = outer_next.astype(jnp.bfloat16)  1.07 us

profile of v1, /device:TPU:0, one launch (start us, length us, event | category | flops | bytes accessed | tf_op | source)
XLA Modules:
  0.0 37.1 jit_solution(15937471649407869696)
XLA Ops:
  0.6 0.0 copy-start
  0.6 1.2 %copy-done = bf16[1,256,2048]{2,1,0:T(8,128)(2,1)S(1)} copy-done((bf16[1,256,2048]{2,1,0:T(8,128)(2,1)S(1)}, bf16[1,256,2048]{2,1,0:T(8,128)(2,1)}, u32[]{:S(2)}) %copy-start) | copy-done | bytes 1048600
  1.9 0.0 copy-start.1
  1.9 1.0 %copy-done.1 = bf16[1,256,1024]{2,1,0:T(8,128)(2,1)S(1)} copy-done((bf16[1,256,1024]{2,1,0:T(8,128)(2,1)S(1)}, bf16[1,256,1024]{2,1,0:T(8,128)(2,1)}, u32[]{:S(2)}) %copy-start.1) | copy-done | bytes 524312
  2.9 0.0 copy-start.2
  2.9 0.0 copy-start.3
  2.9 0.0 copy-start.4
  2.9 0.0 copy-start.5
  2.9 0.0 copy-start.6
  2.9 33.0 %shard_map.94 = f32[64,1024]{1,0:T(8,128)S(1)} custom-call(bf16[256,2048]{1,0:T(8,128)(2,1)S(1)} %bitcast.12, bf16[256,1024]{1,0:T(8,128)(2,1)S(1)} %bitcast.13), custom_call_target="tpu_custom_call" | custom-call | flops 1073741824 | bytes 1835008 | tf_op jit(solution)/shard_map/pallas_call | solution.py:134
  35.9 0.0 copy-done.2
  35.9 0.0 copy-done.3
  35.9 0.0 copy-done.4
  36.0 0.0 copy-done.5
  36.0 0.0 copy-done.6
  36.0 1.1 %fusion.7 = (bf16[64,1024]{1,0:T(8,128)(2,1)}, f32[64,1024]{1,0:T(8,128)}, f32[64,1024]{1,0:T(8,128)}) fusion(f32[64,1024]{1,0:T(8,128)S(1)} %copy-done.2, f32[64,1024]{1,0:T(8,128)S(1)} %copy-done.3, f32[64,1024]{1,0:T(8,128)S(1)} %shard_map.94, f32[1,64,1024]{2,1,0:T(8,128)S(1)} %copy-done.4, f32[1,64,1024]{2,1,0:T(8,128)S(1)} %copy-done.5, ...), kind=kLoop, calls=%fused_computation.11 | loop fusion | flops 1310720 | bytes 2228224 | tf_op jit(solution)/shard_map/convert_element_type | solution.py:184
Async XLA Ops:
  0.6 1.2 %copy-start = (bf16[1,256,2048]{2,1,0:T(8,128)(2,1)S(1)}, bf16[1,256,2048]{2,1,0:T(8,128)(2,1)}, u32[]{:S(2)}) copy-start(bf16[1,256,2048]{2,1,0:T(8,128)(2,1)} %param.7) | copy-start | bytes 3145732
  1.9 1.0 %copy-start.1 = (bf16[1,256,1024]{2,1,0:T(8,128)(2,1)S(1)}, bf16[1,256,1024]{2,1,0:T(8,128)(2,1)}, u32[]{:S(2)}) copy-start(bf16[1,256,1024]{2,1,0:T(8,128)(2,1)} %param.8) | copy-start | bytes 1572868
  2.9 33.0 %copy-start.2 = (f32[64,1024]{1,0:T(8,128)S(1)}, f32[64,1024]{1,0:T(8,128)}, u32[]{:S(2)}) copy-start(f32[64,1024]{1,0:T(8,128)} %param.12) | copy-start | bytes 786436
  2.9 33.0 %copy-start.3 = (f32[64,1024]{1,0:T(8,128)S(1)}, f32[64,1024]{1,0:T(8,128)}, u32[]{:S(2)}) copy-start(f32[64,1024]{1,0:T(8,128)} %param.13) | copy-start | bytes 786436
  2.9 33.0 %copy-start.4 = (f32[1,64,1024]{2,1,0:T(8,128)S(1)}, f32[1,64,1024]{2,1,0:T(8,128)}, u32[]{:S(2)}) copy-start(f32[1,64,1024]{2,1,0:T(8,128)} %param.11) | copy-start | bytes 786436
  2.9 33.1 %copy-start.5 = (f32[1,64,1024]{2,1,0:T(8,128)S(1)}, f32[1,64,1024]{2,1,0:T(8,128)}, u32[]{:S(2)}) copy-start(f32[1,64,1024]{2,1,0:T(8,128)} %param.10) | copy-start | bytes 786436
  2.9 33.1 %copy-start.6 = (f32[1,64,1024]{2,1,0:T(8,128)S(1)}, f32[1,64,1024]{2,1,0:T(8,128)}, u32[]{:S(2)}) copy-start(f32[1,64,1024]{2,1,0:T(8,128)} %param.9) | copy-start | bytes 786436

commit v2 on v1

--- a/solution.py
+++ b/solution.py
@@ -12,13 +12,19 @@
 WIDE = 2 * LANES
 MESH = pl.DeviceIdType.MESH
 
-ORDERS = (
-    (1, 2, 3, 4),
-    (2, 1, 3, 4),
+TALL = (
+    (1, 3, 2, 4),
+    (2, 3, 1, 4),
     (3, 1, 2, 4),
     (3, 2, 1, 4),
-    (1, 2, 3, 4),
-    (2, 1, 3, 4),
+    (1, 2, 4, 3),
+    (2, 1, 4, 3),
+    (1, 4, 2, 3),
+    (2, 4, 1, 3),
+)
+SHORT = (
+    (4, 1, 2, 3),
+    (4, 2, 1, 3),
     (1, 2, 3, 4),
     (2, 1, 3, 4),
 )
@@ -26,8 +32,10 @@
 
 def kernel(
     acts_hbm, cot_hbm, grad_ref,
-    acts, cot, cot_peer, lhs, lhs_peer, part, in0, in1, in2, in3,
-    load_sem, cot_send, cot_recv, lhs_send, lhs_recv, send_sem, recv_sem,
+    acts, cot, cot_peer, lhs, lhs_peer,
+    tall, tall0, tall1, tall2, tall3, short, short0, short1, short2, short3,
+    load_sem, cot_send, cot_recv, lhs_send, lhs_recv,
+    tall_send, tall_recv, short_send, short_recv,
 ):
     me = lax.axis_index("fsdp")
     bit = [lax.rem(me // (1 << b), 2) for b in range(5)]
@@ -37,12 +45,22 @@
     rows, tiles = grad_ref.shape[0], acts.shape[1] // LANES
     groups = 4
     group_rows = lhs.shape[1] // groups
-    pieces, chunks = width // WIDE, width // LANES
-    incoming = (in0, in1, in2, in3)
-
-    load_acts = pltpu.make_async_copy(acts_hbm, acts, load_sem.at[0])
-    load_acts.start()
-    load_cot = pltpu.make_async_copy(cot_hbm, cot, load_sem.at[1])
+    pieces = width // WIDE
+    quarter = rows // 4
+    kinds = (
+        (TALL, tall, (tall0, tall1, tall2, tall3), tall_send, tall_recv),
+        (SHORT, short, (short0, short1, short2, short3), short_send, short_recv),
+    )
+
+    span = acts.shape[1] // groups
+
+    def acts_copy(g):
+        cut = pl.ds(g * span, span)
+        return pltpu.make_async_copy(acts_hbm.at[:, cut], acts.at[:, cut], load_sem.at[g])
+
+    for g in range(groups):
+        acts_copy(g).start()
+    load_cot = pltpu.make_async_copy(cot_hbm, cot, load_sem.at[groups])
     load_cot.start()
     barrier = pltpu.get_barrier_semaphore()
     for b in range(5):
@@ -62,8 +80,9 @@
         cut = pl.ds(g * group_rows, group_rows)
         return to_core(lhs.at[1 - core, cut], lhs_peer.at[cut], lhs_send.at[g], lhs_recv.at[g])
 
-    load_acts.wait()
     for t in range(tiles):
+        if t % (tiles // groups) == 0:
+            acts_copy(t // (tiles // groups)).wait()
         turned = acts[:, t * LANES:(t + 1) * LANES].T
         lhs[0, t * rows:(t + 1) * rows, :] = turned[:rows]
         lhs[1, t * rows:(t + 1) * rows, :] = turned[rows:]
@@ -74,17 +93,22 @@
     for j in range(1, pieces):
         cot_copy(j).start()
 
-    def exchange(c, s):
-        order = ORDERS[c % len(ORDERS)]
+    def exchange(kind, c, s):
+        orders, part, incoming, send, recv = kinds[kind]
+        order = orders[c % len(orders)]
         kept = tuple(bit[b] for b in order[:s])
         return pltpu.make_async_remote_copy(
             src_ref=part.at[(c, *kept, 1 - bit[order[s]])],
             dst_ref=incoming[s].at[c],
-            send_sem=send_sem.at[c, s],
-            recv_sem=recv_sem.at[c, s],
+            send_sem=send.at[c, s],
+            recv_sem=recv.at[c, s],
             device_id={"fsdp": peer[order[s]]},
             device_id_type=MESH,
         )
+
+    def place(kind, c, t):
+        orders = kinds[kind][0]
+        return (c, *((t >> (b - 1)) & 1 for b in orders[c % len(orders)]))
 
     load_cot.wait()
     for j in range(pieces):
@@ -93,37 +117,44 @@
         for g in range(groups):
             if j == 0:
                 lhs_copy(g).wait_recv()
-            block = slice(g * group_rows, (g + 1) * group_rows)
-            product = jnp.dot(lhs[core, block, :], cot[:, cut], preferred_element_type=jnp.float32)
-            product += jnp.dot(lhs_peer[block, :], cot_peer[:, cut], preferred_element_type=jnp.float32)
+            own = slice(g * group_rows, (g + 1) * group_rows)
+            product = jnp.dot(lhs[core, own, :], cot[:, cut], preferred_element_type=jnp.float32)
+            product += jnp.dot(lhs_peer[own, :], cot_peer[:, cut], preferred_element_type=jnp.float32)
             product = product.astype(jnp.bfloat16)
             for k in range(group_rows // rows):
                 t = g * (group_rows // rows) + k
                 for h in range(2):
                     c = 2 * j + h
-                    where = tuple((t >> (b - 1)) & 1 for b in ORDERS[c % len(ORDERS)])
-                    part[(c, *where)] = product[k * rows:(k + 1) * rows, h * LANES:(h + 1) * LANES]
-        exchange(2 * j, 0).start()
-        exchange(2 * j + 1, 0).start()
-
+                    block = product[k * rows:(k + 1) * rows, h * LANES:(h + 1) * LANES]
+                    tall[place(0, c, t)] = block[: 3 * quarter]
+                    short[(*place(1, j, t), pl.ds(h * quarter, quarter))] = block[3 * quarter:]
+        for kind, c in ((0, 2 * j), (0, 2 * j + 1), (1, j)):
+            exchange(kind, c, 0).start()
+
+    every = [item for j in range(pieces) for item in ((0, 2 * j), (0, 2 * j + 1), (1, j))]
     for s in range(4):
-        for c in range(chunks):
-            order = ORDERS[c % len(ORDERS)]
-            exchange(c, s).wait_recv()
+        for kind, c in every:
+            orders, part, incoming = kinds[kind][:3]
+            order = orders[c % len(orders)]
+            exchange(kind, c, s).wait_recv()
             kept = (c, *(bit[b] for b in order[: s + 1]))
             total = part[kept].astype(jnp.float32) + incoming[s][c].astype(jnp.float32)
             if s < 3:
                 part[kept] = total.astype(jnp.bfloat16)
-                exchange(c, s + 1).start()
+                exchange(kind, c, s + 1).start()
+            elif kind == 0:
+                grad_ref[: 3 * quarter, c * LANES:(c + 1) * LANES] = total
             else:
-                grad_ref[:, c * LANES:(c + 1) * LANES] = total
+                for h in range(2):
+                    strip = slice((2 * c + h) * LANES, (2 * c + h + 1) * LANES)
+                    grad_ref[3 * quarter:, strip] = total[h * quarter:(h + 1) * quarter]
     for j in range(pieces):
         cot_copy(j).wait_send()
     for g in range(groups):
         lhs_copy(g).wait_send()
     for s in range(4):
-        for c in range(chunks):
-            exchange(c, s).wait_send()
+        for kind, c in every:
+            exchange(kind, c, s).wait_send()
 
 
 def gradient(tokens, cotangent, devices):
@@ -134,7 +165,7 @@
     return pl.pallas_call(
         kernel,
         out_shape=jax.ShapeDtypeStruct((rows, width), jnp.float32),
-        in_specs=[pl.BlockSpec(memory_space=pl.ANY)] * 2,
+        in_specs=[pl.BlockSpec(memory_space=pltpu.HBM)] * 2,
         out_specs=pl.BlockSpec(memory_space=pltpu.VMEM),
         scratch_shapes=[
             pltpu.VMEM((count, depth), bf16),
@@ -142,21 +173,20 @@
             pltpu.VMEM((count, width), bf16),
             pltpu.VMEM((2, half, count), bf16),
             pltpu.VMEM((half, count), bf16),
-            pltpu.VMEM((chunks, 2, 2, 2, 2, rows, LANES), bf16),
-            pltpu.VMEM((chunks, 2, 2, 2, rows, LANES), bf16),
-            pltpu.VMEM((chunks, 2, 2, rows, LANES), bf16),
-            pltpu.VMEM((chunks, 2, rows, LANES), bf16),
-            pltpu.VMEM((chunks, rows, LANES), bf16),
-            pltpu.SemaphoreType.DMA((2,)),
+            *[pltpu.VMEM((chunks, *[2] * k, 3 * rows // 4, LANES), bf16) for k in (4, 3, 2, 1, 0)],
+            *[pltpu.VMEM((chunks // 2, *[2] * k, rows // 2, LANES), bf16) for k in (4, 3, 2, 1, 0)],
+            pltpu.SemaphoreType.DMA((5,)),
             pltpu.SemaphoreType.DMA((width // WIDE,)),
             pltpu.SemaphoreType.DMA((width // WIDE,)),
             pltpu.SemaphoreType.DMA((4,)),
             pltpu.SemaphoreType.DMA((4,)),
             pltpu.SemaphoreType.DMA((chunks, 4)),
             pltpu.SemaphoreType.DMA((chunks, 4)),
+            pltpu.SemaphoreType.DMA((chunks // 2, 4)),
+            pltpu.SemaphoreType.DMA((chunks // 2, 4)),
         ],
         compiler_params=pltpu.CompilerParams(
-            collective_id=0, has_side_effects=True, vmem_limit_bytes=48 * 1024 * 1024
+            collective_id=0, has_side_effects=True, vmem_limit_bytes=62 * 1024 * 1024
         ),
         cost_estimate=pl.CostEstimate(
             flops=2 * count * depth * width,

time: 37.3 us -> 35.1 us (0.941)
  local copies, waits for them, and re-layouts: 2.28 us -> 0.02 us
  other arithmetic: 1.07 us -> 2.02 us
  Pallas kernels: 33 us -> 32.1 us
    unnamed x14 -> x10, local copies, waits for them, and re-layouts: 2.28 us -> 0.02 us
    convert_element_type x1, other arithmetic: 1.07 us -> 2.02 us  [shards(): weight_next = outer_next.astype(jnp.bfloat16)]
    pallas_call x1, Pallas kernels: 33 us -> 32.1 us  [gradient(): pl.pallas_call(kernel, out_shape=jax.ShapeDtypeStruct((rows, width), jnp....]
where the time goes in v2:
time: 35.1 us; the launch traced here: 34.9 us
  Pallas kernels  32.1 us (91%)
  other arithmetic  2.02 us (6%)
  between operations  0.72 us (2%)
    pallas_call x1, Pallas kernels, gradient(): pl.pallas_call(kernel, out_shape=jax.ShapeDtypeStruct((rows, width), jnp....  32.1 us
    convert_element_type x1, other arithmetic, shards(): weight_next = outer_next.astype(jnp.bfloat16)  2.02 us

profile of v2, /device:TPU:0, one launch (start us, length us, event | category | flops | bytes accessed | tf_op | source)
XLA Modules:
  0.0 34.9 jit_solution(7246654019949680572)
XLA Ops:
  0.6 0.0 copy-start
  0.6 0.0 copy-start.1
  0.7 0.0 copy-start.2
  0.7 0.0 copy-start.3
  0.7 0.0 copy-start.4
  0.7 32.1 %shard_map.94 = f32[64,1024]{1,0:T(8,128)} custom-call(bf16[256,2048]{1,0:T(8,128)(2,1)} %bitcast.12, bf16[256,1024]{1,0:T(8,128)(2,1)} %bitcast.13), custom_call_target="tpu_custom_call" | custom-call | flops 1073741824 | bytes 1835008 | tf_op jit(solution)/shard_map/pallas_call | solution.py:165
  32.8 0.0 copy-done
  32.8 0.0 copy-done.1
  32.8 0.0 copy-done.2
  32.9 0.0 copy-done.3
  32.9 0.0 copy-done.4
  32.9 2.0 %fusion.7 = (bf16[64,1024]{1,0:T(8,128)(2,1)}, f32[64,1024]{1,0:T(8,128)}, f32[64,1024]{1,0:T(8,128)}) fusion(f32[64,1024]{1,0:T(8,128)S(1)} %copy-done, f32[64,1024]{1,0:T(8,128)S(1)} %copy-done.1, f32[64,1024]{1,0:T(8,128)} %shard_map.94, f32[1,64,1024]{2,1,0:T(8,128)S(1)} %copy-done.2, f32[1,64,1024]{2,1,0:T(8,128)S(1)} %copy-done.3, ...), kind=kLoop, calls=%fused_computation.11 | loop fusion | flops 1310720 | bytes 2228224 | tf_op jit(solution)/shard_map/convert_element_type | solution.py:214
Async XLA Ops:
  0.6 32.2 %copy-start = (f32[64,1024]{1,0:T(8,128)S(1)}, f32[64,1024]{1,0:T(8,128)}, u32[]{:S(2)}) copy-start(f32[64,1024]{1,0:T(8,128)} %param.12) | copy-start | bytes 786436
  0.6 32.2 %copy-start.1 = (f32[64,1024]{1,0:T(8,128)S(1)}, f32[64,1024]{1,0:T(8,128)}, u32[]{:S(2)}) copy-start(f32[64,1024]{1,0:T(8,128)} %param.13) | copy-start | bytes 786436
  0.7 32.2 %copy-start.2 = (f32[1,64,1024]{2,1,0:T(8,128)S(1)}, f32[1,64,1024]{2,1,0:T(8,128)}, u32[]{:S(2)}) copy-start(f32[1,64,1024]{2,1,0:T(8,128)} %param.11) | copy-start | bytes 786436
  0.7 32.2 %copy-start.3 = (f32[1,64,1024]{2,1,0:T(8,128)S(1)}, f32[1,64,1024]{2,1,0:T(8,128)}, u32[]{:S(2)}) copy-start(f32[1,64,1024]{2,1,0:T(8,128)} %param.10) | copy-start | bytes 786436
  0.7 32.2 %copy-start.4 = (f32[1,64,1024]{2,1,0:T(8,128)S(1)}, f32[1,64,1024]{2,1,0:T(8,128)}, u32[]{:S(2)}) copy-start(f32[1,64,1024]{2,1,0:T(8,128)} %param.9) | copy-start | bytes 786436

commit v3 on v2

--- a/solution.py
+++ b/solution.py
@@ -16,18 +16,21 @@
     (1, 3, 2, 4),
     (2, 3, 1, 4),
     (3, 1, 2, 4),
+    (1, 2, 4, 3),
     (3, 2, 1, 4),
-    (1, 2, 4, 3),
     (2, 1, 4, 3),
     (1, 4, 2, 3),
     (2, 4, 1, 3),
 )
 SHORT = (
     (4, 1, 2, 3),
+    (2, 1, 3, 4),
     (4, 2, 1, 3),
     (1, 2, 3, 4),
-    (2, 1, 3, 4),
 )
+LEAD = ((0, 0), (0, 1), (0, 2), (1, 1), (1, 0), (0, 3))
+FOLLOW = ((0, 6), (0, 5), (0, 4), (0, 7), (1, 2), (1, 3))
+ROUNDS = ((LEAD, 0), (LEAD, 1), (FOLLOW, 0), (LEAD, 2), (FOLLOW, 1), (LEAD, 3), (FOLLOW, 2), (FOLLOW, 3))
 
 
 def kernel(
@@ -110,50 +113,62 @@
         orders = kinds[kind][0]
         return (c, *((t >> (b - 1)) & 1 for b in orders[c % len(orders)]))
 
+    def finish(kind, c, s):
+        orders, part, incoming = kinds[kind][:3]
+        order = orders[c % len(orders)]
+        kept = (c, *(bit[b] for b in order[: s + 1]))
+        total = part[kept].astype(jnp.float32) + incoming[s][c].astype(jnp.float32)
+        if s < 3:
+            part[kept] = total.astype(jnp.bfloat16)
+            exchange(kind, c, s + 1).start()
+        elif kind == 0:
+            grad_ref[: 3 * quarter, c * LANES:(c + 1) * LANES] = total
+        else:
+            for h in range(2):
+                strip = slice((2 * c + h) * LANES, (2 * c + h + 1) * LANES)
+                grad_ref[3 * quarter:, strip] = total[h * quarter:(h + 1) * quarter]
+
+    def multiply(left, right):
+        return jnp.dot(left, right, preferred_element_type=jnp.float32)
+
     load_cot.wait()
     for j in range(pieces):
         cut = slice(j * WIDE, (j + 1) * WIDE)
+        block = [slice(g * group_rows, (g + 1) * group_rows) for g in range(groups)]
+        if j == 0:
+            ours = [multiply(lhs[core, block[g], :], cot[:, cut]) for g in range(groups)]
         cot_copy(j).wait_recv()
         for g in range(groups):
             if j == 0:
                 lhs_copy(g).wait_recv()
-            own = slice(g * group_rows, (g + 1) * group_rows)
-            product = jnp.dot(lhs[core, own, :], cot[:, cut], preferred_element_type=jnp.float32)
-            product += jnp.dot(lhs_peer[own, :], cot_peer[:, cut], preferred_element_type=jnp.float32)
+                product = ours[g]
+            else:
+                product = multiply(lhs[core, block[g], :], cot[:, cut])
+            product += multiply(lhs_peer[block[g], :], cot_peer[:, cut])
             product = product.astype(jnp.bfloat16)
             for k in range(group_rows // rows):
                 t = g * (group_rows // rows) + k
                 for h in range(2):
                     c = 2 * j + h
-                    block = product[k * rows:(k + 1) * rows, h * LANES:(h + 1) * LANES]
-                    tall[place(0, c, t)] = block[: 3 * quarter]
-                    short[(*place(1, j, t), pl.ds(h * quarter, quarter))] = block[3 * quarter:]
+                    cell = product[k * rows:(k + 1) * rows, h * LANES:(h + 1) * LANES]
+                    tall[place(0, c, t)] = cell[: 3 * quarter]
+                    short[(*place(1, j, t), pl.ds(h * quarter, quarter))] = cell[3 * quarter:]
         for kind, c in ((0, 2 * j), (0, 2 * j + 1), (1, j)):
-            exchange(kind, c, 0).start()
-
-    every = [item for j in range(pieces) for item in ((0, 2 * j), (0, 2 * j + 1), (1, j))]
-    for s in range(4):
-        for kind, c in every:
-            orders, part, incoming = kinds[kind][:3]
-            order = orders[c % len(orders)]
+            if (kind, c) in LEAD:
+                exchange(kind, c, 0).start()
+
+    for members, s in ROUNDS:
+        for (kind, c), follower in zip(members, FOLLOW):
             exchange(kind, c, s).wait_recv()
-            kept = (c, *(bit[b] for b in order[: s + 1]))
-            total = part[kept].astype(jnp.float32) + incoming[s][c].astype(jnp.float32)
-            if s < 3:
-                part[kept] = total.astype(jnp.bfloat16)
-                exchange(kind, c, s + 1).start()
-            elif kind == 0:
-                grad_ref[: 3 * quarter, c * LANES:(c + 1) * LANES] = total
-            else:
-                for h in range(2):
-                    strip = slice((2 * c + h) * LANES, (2 * c + h + 1) * LANES)
-                    grad_ref[3 * quarter:, strip] = total[h * quarter:(h + 1) * quarter]
+            if members is LEAD and s == 0:
+                exchange(*follower, 0).start()
+            finish(kind, c, s)
     for j in range(pieces):
         cot_copy(j).wait_send()
     for g in range(groups):
         lhs_copy(g).wait_send()
     for s in range(4):
-        for kind, c in every:
+        for kind, c in LEAD + FOLLOW:
             exchange(kind, c, s).wait_send()
 
 

time: 35.1 us -> 39.4 us (1.12)
  Pallas kernels: 32.1 us -> 36.4 us
    pallas_call x1, Pallas kernels: 32.1 us -> 36.4 us  [gradient(): pl.pallas_call(kernel, out_shape=jax.ShapeDtypeStruct((rows, width), jnp....]
where the time goes in v3:
time: 39.4 us; the launch traced here: 39.2 us
  Pallas kernels  36.4 us (92%)
  other arithmetic  2.02 us (5%)
  between operations  0.72 us (2%)
    pallas_call x1, Pallas kernels, gradient(): pl.pallas_call(kernel, out_shape=jax.ShapeDtypeStruct((rows, width), jnp....  36.4 us
    convert_element_type x1, other arithmetic, shards(): weight_next = outer_next.astype(jnp.bfloat16)  2.02 us

profile of v3, /device:TPU:0, one launch (start us, length us, event | category | flops | bytes accessed | tf_op | source)
XLA Modules:
  0.0 39.2 jit_solution(11188666489671921878)
XLA Ops:
  0.6 0.0 copy-start
  0.6 0.0 copy-start.1
  0.7 0.0 copy-start.2
  0.7 0.0 copy-start.3
  0.7 0.0 copy-start.4
  0.7 36.4 %shard_map.94 = f32[64,1024]{1,0:T(8,128)} custom-call(bf16[256,2048]{1,0:T(8,128)(2,1)} %bitcast.12, bf16[256,1024]{1,0:T(8,128)(2,1)} %bitcast.13), custom_call_target="tpu_custom_call" | custom-call | flops 1073741824 | bytes 1835008 | tf_op jit(solution)/shard_map/pallas_call | solution.py:180
  37.1 0.0 copy-done
  37.1 0.0 copy-done.1
  37.2 0.0 copy-done.2
  37.2 0.0 copy-done.3
  37.2 0.0 copy-done.4
  37.2 2.0 %fusion.7 = (bf16[64,1024]{1,0:T(8,128)(2,1)}, f32[64,1024]{1,0:T(8,128)}, f32[64,1024]{1,0:T(8,128)}) fusion(f32[64,1024]{1,0:T(8,128)S(1)} %copy-done, f32[64,1024]{1,0:T(8,128)S(1)} %copy-done.1, f32[64,1024]{1,0:T(8,128)} %shard_map.94, f32[1,64,1024]{2,1,0:T(8,128)S(1)} %copy-done.2, f32[1,64,1024]{2,1,0:T(8,128)S(1)} %copy-done.3, ...), kind=kLoop, calls=%fused_computation.11 | loop fusion | flops 1310720 | bytes 2228224 | tf_op jit(solution)/shard_map/convert_element_type | solution.py:229
Async XLA Ops:
  0.6 36.5 %copy-start = (f32[64,1024]{1,0:T(8,128)S(1)}, f32[64,1024]{1,0:T(8,128)}, u32[]{:S(2)}) copy-start(f32[64,1024]{1,0:T(8,128)} %param.12) | copy-start | bytes 786436
  0.6 36.5 %copy-start.1 = (f32[64,1024]{1,0:T(8,128)S(1)}, f32[64,1024]{1,0:T(8,128)}, u32[]{:S(2)}) copy-start(f32[64,1024]{1,0:T(8,128)} %param.13) | copy-start | bytes 786436
  0.7 36.5 %copy-start.2 = (f32[1,64,1024]{2,1,0:T(8,128)S(1)}, f32[1,64,1024]{2,1,0:T(8,128)}, u32[]{:S(2)}) copy-start(f32[1,64,1024]{2,1,0:T(8,128)} %param.11) | copy-start | bytes 786436
  0.7 36.5 %copy-start.3 = (f32[1,64,1024]{2,1,0:T(8,128)S(1)}, f32[1,64,1024]{2,1,0:T(8,128)}, u32[]{:S(2)}) copy-start(f32[1,64,1024]{2,1,0:T(8,128)} %param.10) | copy-start | bytes 786436
  0.7 36.5 %copy-start.4 = (f32[1,64,1024]{2,1,0:T(8,128)S(1)}, f32[1,64,1024]{2,1,0:T(8,128)}, u32[]{:S(2)}) copy-start(f32[1,64,1024]{2,1,0:T(8,128)} %param.9) | copy-start | bytes 786436

commit v4 on v3

--- a/solution.py
+++ b/solution.py
@@ -13,29 +13,36 @@
 MESH = pl.DeviceIdType.MESH
 
 TALL = (
-    (1, 3, 2, 4),
+    (1, 4, 2, 3),
     (2, 3, 1, 4),
+    (3, 2, 4, 1),
+    (4, 2, 1, 3),
+    (1, 2, 4, 3),
     (3, 1, 2, 4),
-    (1, 2, 4, 3),
-    (3, 2, 1, 4),
-    (2, 1, 4, 3),
-    (1, 4, 2, 3),
-    (2, 4, 1, 3),
+    (1, 2, 3, 4),
+    (2, 1, 3, 4),
 )
 SHORT = (
     (4, 1, 2, 3),
     (2, 1, 3, 4),
-    (4, 2, 1, 3),
-    (1, 2, 3, 4),
+    (2, 1, 3, 4),
+    (1, 2, 4, 3),
 )
-LEAD = ((0, 0), (0, 1), (0, 2), (1, 1), (1, 0), (0, 3))
-FOLLOW = ((0, 6), (0, 5), (0, 4), (0, 7), (1, 2), (1, 3))
-ROUNDS = ((LEAD, 0), (LEAD, 1), (FOLLOW, 0), (LEAD, 2), (FOLLOW, 1), (LEAD, 3), (FOLLOW, 2), (FOLLOW, 3))
+ARRIVALS = (
+    (0, 0, 0), (0, 1, 0), (1, 0, 0), (0, 2, 0), (1, 1, 0), (0, 4, 0),
+    (1, 2, 0), (0, 6, 0), (0, 7, 0), (0, 3, 0), (0, 5, 0), (1, 3, 0),
+    (0, 2, 1), (1, 0, 1), (1, 1, 1), (0, 4, 1), (0, 0, 1), (0, 1, 1),
+    (1, 2, 1), (0, 6, 1), (1, 1, 2), (0, 2, 2), (0, 7, 1), (0, 3, 1),
+    (1, 2, 2), (0, 4, 2), (0, 5, 1), (1, 3, 1), (1, 0, 2), (0, 6, 2),
+    (0, 1, 2), (1, 1, 3), (0, 2, 3), (0, 0, 2), (0, 7, 2), (0, 3, 2),
+    (1, 2, 3), (0, 4, 3), (0, 5, 2), (1, 0, 3), (1, 3, 2), (0, 6, 3),
+    (0, 1, 3), (0, 0, 3), (0, 7, 3), (0, 3, 3), (1, 3, 3), (0, 5, 3),
+)
 
 
 def kernel(
     acts_hbm, cot_hbm, grad_ref,
-    acts, cot, cot_peer, lhs, lhs_peer,
+    acts, cot, lhs,
     tall, tall0, tall1, tall2, tall3, short, short0, short1, short2, short3,
     load_sem, cot_send, cot_recv, lhs_send, lhs_recv,
     tall_send, tall_recv, short_send, short_recv,
@@ -44,7 +51,7 @@
     bit = [lax.rem(me // (1 << b), 2) for b in range(5)]
     peer = [me + (1 - 2 * bit[b]) * (1 << b) for b in range(5)]
     core = bit[0]
-    tokens, width = cot.shape
+    tokens, width = acts.shape[0], cot.shape[1]
     rows, tiles = grad_ref.shape[0], acts.shape[1] // LANES
     groups = 4
     group_rows = lhs.shape[1] // groups
@@ -63,7 +70,7 @@
 
     for g in range(groups):
         acts_copy(g).start()
-    load_cot = pltpu.make_async_copy(cot_hbm, cot, load_sem.at[groups])
+    load_cot = pltpu.make_async_copy(cot_hbm, cot.at[:tokens], load_sem.at[groups])
     load_cot.start()
     barrier = pltpu.get_barrier_semaphore()
     for b in range(5):
@@ -77,18 +84,21 @@
 
     def cot_copy(j):
         cut = pl.ds(j * WIDE, WIDE)
-        return to_core(cot_hbm.at[:, cut], cot_peer.at[:, cut], cot_send.at[j], cot_recv.at[j])
+        return to_core(cot_hbm.at[:, cut], cot.at[tokens:, cut], cot_send.at[j], cot_recv.at[j])
 
     def lhs_copy(g):
         cut = pl.ds(g * group_rows, group_rows)
-        return to_core(lhs.at[1 - core, cut], lhs_peer.at[cut], lhs_send.at[g], lhs_recv.at[g])
+        return to_core(
+            lhs.at[1 - core, cut, :tokens], lhs.at[1 - core, cut, tokens:],
+            lhs_send.at[g], lhs_recv.at[g],
+        )
 
     for t in range(tiles):
         if t % (tiles // groups) == 0:
             acts_copy(t // (tiles // groups)).wait()
         turned = acts[:, t * LANES:(t + 1) * LANES].T
-        lhs[0, t * rows:(t + 1) * rows, :] = turned[:rows]
-        lhs[1, t * rows:(t + 1) * rows, :] = turned[rows:]
+        lhs[0, t * rows:(t + 1) * rows, :tokens] = turned[:rows]
+        lhs[1, t * rows:(t + 1) * rows, :tokens] = turned[rows:]
     pl.semaphore_wait(barrier, 5)
     cot_copy(0).start()
     for g in range(groups):
@@ -128,48 +138,32 @@
                 strip = slice((2 * c + h) * LANES, (2 * c + h + 1) * LANES)
                 grad_ref[3 * quarter:, strip] = total[h * quarter:(h + 1) * quarter]
 
-    def multiply(left, right):
-        return jnp.dot(left, right, preferred_element_type=jnp.float32)
-
     load_cot.wait()
+    for g in range(groups):
+        lhs_copy(g).wait_recv()
     for j in range(pieces):
-        cut = slice(j * WIDE, (j + 1) * WIDE)
-        block = [slice(g * group_rows, (g + 1) * group_rows) for g in range(groups)]
-        if j == 0:
-            ours = [multiply(lhs[core, block[g], :], cot[:, cut]) for g in range(groups)]
         cot_copy(j).wait_recv()
-        for g in range(groups):
-            if j == 0:
-                lhs_copy(g).wait_recv()
-                product = ours[g]
-            else:
-                product = multiply(lhs[core, block[g], :], cot[:, cut])
-            product += multiply(lhs_peer[block[g], :], cot_peer[:, cut])
-            product = product.astype(jnp.bfloat16)
-            for k in range(group_rows // rows):
-                t = g * (group_rows // rows) + k
-                for h in range(2):
-                    c = 2 * j + h
-                    cell = product[k * rows:(k + 1) * rows, h * LANES:(h + 1) * LANES]
-                    tall[place(0, c, t)] = cell[: 3 * quarter]
-                    short[(*place(1, j, t), pl.ds(h * quarter, quarter))] = cell[3 * quarter:]
+        product = jnp.dot(
+            lhs[core], cot[:, j * WIDE:(j + 1) * WIDE], preferred_element_type=jnp.float32
+        ).astype(jnp.bfloat16)
+        for t in range(tiles):
+            for h in range(2):
+                c = 2 * j + h
+                cell = product[t * rows:(t + 1) * rows, h * LANES:(h + 1) * LANES]
+                tall[place(0, c, t)] = cell[: 3 * quarter]
+                short[(*place(1, j, t), pl.ds(h * quarter, quarter))] = cell[3 * quarter:]
         for kind, c in ((0, 2 * j), (0, 2 * j + 1), (1, j)):
-            if (kind, c) in LEAD:
-                exchange(kind, c, 0).start()
-
-    for members, s in ROUNDS:
-        for (kind, c), follower in zip(members, FOLLOW):
-            exchange(kind, c, s).wait_recv()
-            if members is LEAD and s == 0:
-                exchange(*follower, 0).start()
-            finish(kind, c, s)
+            exchange(kind, c, 0).start()
+
+    for kind, c, s in ARRIVALS:
+        exchange(kind, c, s).wait_recv()
+        finish(kind, c, s)
     for j in range(pieces):
         cot_copy(j).wait_send()
     for g in range(groups):
         lhs_copy(g).wait_send()
-    for s in range(4):
-        for kind, c in LEAD + FOLLOW:
-            exchange(kind, c, s).wait_send()
+    for kind, c, s in ARRIVALS:
+        exchange(kind, c, s).wait_send()
 
 
 def gradient(tokens, cotangent, devices):
@@ -184,10 +178,8 @@
         out_specs=pl.BlockSpec(memory_space=pltpu.VMEM),
         scratch_shapes=[
             pltpu.VMEM((count, depth), bf16),
-            pltpu.VMEM((count, width), bf16),
-            pltpu.VMEM((count, width), bf16),
-            pltpu.VMEM((2, half, count), bf16),
-            pltpu.VMEM((half, count), bf16),
+            pltpu.VMEM((2 * count, width), bf16),
+            pltpu.VMEM((2, half, 2 * count), bf16),
             *[pltpu.VMEM((chunks, *[2] * k, 3 * rows // 4, LANES), bf16) for k in (4, 3, 2, 1, 0)],
             *[pltpu.VMEM((chunks // 2, *[2] * k, rows // 2, LANES), bf16) for k in (4, 3, 2, 1, 0)],
             pltpu.SemaphoreType.DMA((5,)),

time: 39.4 us -> 34.4 us (0.87)
  Pallas kernels: 36.4 us -> 31.5 us
    pallas_call x1, Pallas kernels: 36.4 us -> 31.5 us  [gradient(): pl.pallas_call(kernel, out_shape=jax.ShapeDtypeStruct((rows, width), jnp....]
where the time goes in v4:
time: 34.4 us; the launch traced here: 34.2 us
  Pallas kernels  31.5 us (92%)
  other arithmetic  2.02 us (6%)
  between operations  0.72 us (2%)
    pallas_call x1, Pallas kernels, gradient(): pl.pallas_call(kernel, out_shape=jax.ShapeDtypeStruct((rows, width), jnp....  31.5 us
    convert_element_type x1, other arithmetic, shards(): weight_next = outer_next.astype(jnp.bfloat16)  2.02 us

profile of v4, /device:TPU:0, one launch (start us, length us, event | category | flops | bytes accessed | tf_op | source)
XLA Modules:
  0.0 34.2 jit_solution(17615090959396010025)
XLA Ops:
  0.6 0.0 copy-start
  0.6 0.0 copy-start.1
  0.7 0.0 copy-start.2
  0.7 0.0 copy-start.3
  0.7 0.0 copy-start.4
  0.7 31.5 %shard_map.94 = f32[64,1024]{1,0:T(8,128)} custom-call(bf16[256,2048]{1,0:T(8,128)(2,1)} %bitcast.12, bf16[256,1024]{1,0:T(8,128)(2,1)} %bitcast.13), custom_call_target="tpu_custom_call" | custom-call | flops 1073741824 | bytes 1835008 | tf_op jit(solution)/shard_map/pallas_call | solution.py:174
  32.1 0.0 copy-done
  32.2 0.0 copy-done.1
  32.2 0.0 copy-done.2
  32.2 0.0 copy-done.3
  32.2 0.0 copy-done.4
  32.2 2.0 %fusion.7 = (bf16[64,1024]{1,0:T(8,128)(2,1)}, f32[64,1024]{1,0:T(8,128)}, f32[64,1024]{1,0:T(8,128)}) fusion(f32[64,1024]{1,0:T(8,128)S(1)} %copy-done, f32[64,1024]{1,0:T(8,128)S(1)} %copy-done.1, f32[64,1024]{1,0:T(8,128)} %shard_map.94, f32[1,64,1024]{2,1,0:T(8,128)S(1)} %copy-done.2, f32[1,64,1024]{2,1,0:T(8,128)S(1)} %copy-done.3, ...), kind=kLoop, calls=%fused_computation.11 | loop fusion | flops 1310720 | bytes 2228224 | tf_op jit(solution)/shard_map/convert_element_type | solution.py:221
Async XLA Ops:
  0.6 31.5 %copy-start = (f32[64,1024]{1,0:T(8,128)S(1)}, f32[64,1024]{1,0:T(8,128)}, u32[]{:S(2)}) copy-start(f32[64,1024]{1,0:T(8,128)} %param.12) | copy-start | bytes 786436
  0.6 31.5 %copy-start.1 = (f32[64,1024]{1,0:T(8,128)S(1)}, f32[64,1024]{1,0:T(8,128)}, u32[]{:S(2)}) copy-start(f32[64,1024]{1,0:T(8,128)} %param.13) | copy-start | bytes 786436
  0.7 31.5 %copy-start.2 = (f32[1,64,1024]{2,1,0:T(8,128)S(1)}, f32[1,64,1024]{2,1,0:T(8,128)}, u32[]{:S(2)}) copy-start(f32[1,64,1024]{2,1,0:T(8,128)} %param.11) | copy-start | bytes 786436
  0.7 31.5 %copy-start.3 = (f32[1,64,1024]{2,1,0:T(8,128)S(1)}, f32[1,64,1024]{2,1,0:T(8,128)}, u32[]{:S(2)}) copy-start(f32[1,64,1024]{2,1,0:T(8,128)} %param.10) | copy-start | bytes 786436
  0.7 31.5 %copy-start.4 = (f32[1,64,1024]{2,1,0:T(8,128)S(1)}, f32[1,64,1024]{2,1,0:T(8,128)}, u32[]{:S(2)}) copy-start(f32[1,64,1024]{2,1,0:T(8,128)} %param.9) | copy-start | bytes 786436

commit v5 on v4

--- a/solution.py
+++ b/solution.py
@@ -13,43 +13,53 @@
 MESH = pl.DeviceIdType.MESH
 
 TALL = (
-    (1, 4, 2, 3),
-    (2, 3, 1, 4),
-    (3, 2, 4, 1),
-    (4, 2, 1, 3),
-    (1, 2, 4, 3),
-    (3, 1, 2, 4),
-    (1, 2, 3, 4),
-    (2, 1, 3, 4),
+    ((4,), (1,), (2,), (3,)),
+    ((2,), (1,), (4,), (3,)),
+    ((3,), (1, 2), (4,)),
+    ((2,), (3,), (1,), (4,)),
+    ((1,), (2,), (3, 4)),
+    ((2,), (1,), (3, 4)),
+    ((1,), (2,), (3, 4)),
+    ((3,), (1, 2), (4,)),
 )
 SHORT = (
-    (4, 1, 2, 3),
-    (2, 1, 3, 4),
-    (2, 1, 3, 4),
-    (1, 2, 4, 3),
+    ((3,), (4,), (1,), (2,)),
+    ((1,), (2,), (3, 4)),
+    ((4,), (1,), (3,), (2,)),
+    ((1,), (2,), (3,), (4,)),
 )
 ARRIVALS = (
-    (0, 0, 0), (0, 1, 0), (1, 0, 0), (0, 2, 0), (1, 1, 0), (0, 4, 0),
-    (1, 2, 0), (0, 6, 0), (0, 7, 0), (0, 3, 0), (0, 5, 0), (1, 3, 0),
-    (0, 2, 1), (1, 0, 1), (1, 1, 1), (0, 4, 1), (0, 0, 1), (0, 1, 1),
-    (1, 2, 1), (0, 6, 1), (1, 1, 2), (0, 2, 2), (0, 7, 1), (0, 3, 1),
-    (1, 2, 2), (0, 4, 2), (0, 5, 1), (1, 3, 1), (1, 0, 2), (0, 6, 2),
-    (0, 1, 2), (1, 1, 3), (0, 2, 3), (0, 0, 2), (0, 7, 2), (0, 3, 2),
-    (1, 2, 3), (0, 4, 3), (0, 5, 2), (1, 0, 3), (1, 3, 2), (0, 6, 3),
-    (0, 1, 3), (0, 0, 3), (0, 7, 3), (0, 3, 3), (1, 3, 3), (0, 5, 3),
+    (1, 1, 0), (0, 1, 0), (1, 0, 0), (0, 3, 0), (1, 3, 0), (0, 5, 0),
+    (1, 1, 1), (0, 4, 0), (1, 2, 0), (0, 6, 0), (0, 0, 0), (0, 1, 1),
+    (1, 3, 1), (0, 2, 0), (0, 5, 1), (1, 1, 2), (0, 7, 0), (1, 2, 1),
+    (0, 4, 1), (1, 0, 1), (0, 6, 1), (0, 0, 1), (0, 3, 1), (1, 3, 2),
+    (0, 1, 2), (0, 2, 1), (0, 5, 2), (0, 7, 1), (1, 0, 2), (0, 0, 2),
+    (0, 3, 2), (1, 2, 2), (0, 4, 2), (1, 3, 3), (0, 6, 2), (0, 1, 3),
+    (1, 0, 3), (0, 2, 2), (0, 7, 2), (0, 0, 3), (1, 2, 3), (0, 3, 3),
 )
+
+
+def flips(block):
+    return [
+        tuple(b for i, b in enumerate(block) if mask >> i & 1) for mask in range(1, 1 << len(block))
+    ]
 
 
 def kernel(
     acts_hbm, cot_hbm, grad_ref,
     acts, cot, lhs,
-    tall, tall0, tall1, tall2, tall3, short, short0, short1, short2, short3,
+    tall, tall_in, short, short_in,
     load_sem, cot_send, cot_recv, lhs_send, lhs_recv,
     tall_send, tall_recv, short_send, short_recv,
 ):
     me = lax.axis_index("fsdp")
     bit = [lax.rem(me // (1 << b), 2) for b in range(5)]
-    peer = [me + (1 - 2 * bit[b]) * (1 << b) for b in range(5)]
+    step = [(1 - 2 * bit[b]) * (1 << b) for b in range(5)]
+    partners = sorted({p for rounds in TALL + SHORT for block in rounds for p in flips(block)})
+
+    def device(flipped):
+        return {"fsdp": me + sum(step[b] for b in flipped)}
+
     core = bit[0]
     tokens, width = acts.shape[0], cot.shape[1]
     rows, tiles = grad_ref.shape[0], acts.shape[1] // LANES
@@ -58,8 +68,8 @@
     pieces = width // WIDE
     quarter = rows // 4
     kinds = (
-        (TALL, tall, (tall0, tall1, tall2, tall3), tall_send, tall_recv),
-        (SHORT, short, (short0, short1, short2, short3), short_send, short_recv),
+        (TALL, tall, tall_in, tall_send, tall_recv),
+        (SHORT, short, short_in, short_send, short_recv),
     )
 
     span = acts.shape[1] // groups
@@ -73,13 +83,13 @@
     load_cot = pltpu.make_async_copy(cot_hbm, cot.at[:tokens], load_sem.at[groups])
     load_cot.start()
     barrier = pltpu.get_barrier_semaphore()
-    for b in range(5):
-        pl.semaphore_signal(barrier, inc=1, device_id={"fsdp": peer[b]}, device_id_type=MESH)
+    for flipped in [(0,)] + partners:
+        pl.semaphore_signal(barrier, inc=1, device_id=device(flipped), device_id_type=MESH)
 
     def to_core(src, dst, send, recv):
         return pltpu.make_async_remote_copy(
             src_ref=src, dst_ref=dst, send_sem=send, recv_sem=recv,
-            device_id={"fsdp": peer[0]}, device_id_type=MESH,
+            device_id=device((0,)), device_id_type=MESH,
         )
 
     def cot_copy(j):
@@ -99,38 +109,59 @@
         turned = acts[:, t * LANES:(t + 1) * LANES].T
         lhs[0, t * rows:(t + 1) * rows, :tokens] = turned[:rows]
         lhs[1, t * rows:(t + 1) * rows, :tokens] = turned[rows:]
-    pl.semaphore_wait(barrier, 5)
+    pl.semaphore_wait(barrier, 1 + len(partners))
     cot_copy(0).start()
     for g in range(groups):
         lhs_copy(g).start()
     for j in range(1, pieces):
         cot_copy(j).start()
 
-    def exchange(kind, c, s):
-        orders, part, incoming, send, recv = kinds[kind]
-        order = orders[c % len(orders)]
-        kept = tuple(bit[b] for b in order[:s])
-        return pltpu.make_async_remote_copy(
-            src_ref=part.at[(c, *kept, 1 - bit[order[s]])],
-            dst_ref=incoming[s].at[c],
-            send_sem=send.at[c, s],
-            recv_sem=recv.at[c, s],
-            device_id={"fsdp": peer[order[s]]},
-            device_id_type=MESH,
-        )
+    def exchanges(kind, c, s):
+        rounds, part, incoming, send, recv = kinds[kind]
+        rounds = rounds[c % len(rounds)]
+        done = [b for block in rounds[:s] for b in block]
+        slot, count, copies = 16 - (16 >> len(done)), 16 >> (len(done) + len(rounds[s])), []
+        sem = sum(len(flips(block)) for block in rounds[:s])
+        for flipped in flips(rounds[s]):
+            start = 0
+            for i, b in enumerate(done + list(rounds[s])):
+                start += (1 - bit[b] if b in flipped else bit[b]) * (8 >> i)
+            copies.append(pltpu.make_async_remote_copy(
+                src_ref=part.at[c, pl.ds(start, count)],
+                dst_ref=incoming.at[c, pl.ds(slot, count)],
+                send_sem=send.at[c, sem],
+                recv_sem=recv.at[c, sem],
+                device_id=device(flipped),
+                device_id_type=MESH,
+            ))
+            slot, sem = slot + count, sem + 1
+        return copies
 
     def place(kind, c, t):
-        orders = kinds[kind][0]
-        return (c, *((t >> (b - 1)) & 1 for b in orders[c % len(orders)]))
+        rounds = kinds[kind][0]
+        bits = [b for block in rounds[c % len(rounds)] for b in block]
+        return c, sum((t >> (b - 1) & 1) * (8 >> i) for i, b in enumerate(bits))
 
     def finish(kind, c, s):
-        orders, part, incoming = kinds[kind][:3]
-        order = orders[c % len(orders)]
-        kept = (c, *(bit[b] for b in order[: s + 1]))
-        total = part[kept].astype(jnp.float32) + incoming[s][c].astype(jnp.float32)
-        if s < 3:
-            part[kept] = total.astype(jnp.bfloat16)
-            exchange(kind, c, s + 1).start()
+        rounds, part, incoming = kinds[kind][:3]
+        rounds = rounds[c % len(rounds)]
+        done = [b for block in rounds[:s] for b in block]
+        slot = 16 - (16 >> len(done))
+        count = 16 >> (len(done) + len(rounds[s]))
+        start = sum(bit[b] * (8 >> i) for i, b in enumerate(done + list(rounds[s])))
+        kept = (c, pl.ds(start, count))
+        terms = [part[kept]]
+        for i in range(len(flips(rounds[s]))):
+            terms.append(incoming[c, slot + i * count:slot + (i + 1) * count])
+        if s + 1 == len(rounds):
+            terms = [term[0].astype(jnp.float32) for term in terms]
+        while len(terms) > 1:
+            terms = [sum(terms[i + 1:i + 2], terms[i]) for i in range(0, len(terms), 2)]
+        total = terms[0]
+        if s + 1 < len(rounds):
+            part[kept] = total
+            for copy in exchanges(kind, c, s + 1):
+                copy.start()
         elif kind == 0:
             grad_ref[: 3 * quarter, c * LANES:(c + 1) * LANES] = total
         else:
@@ -153,17 +184,20 @@
                 tall[place(0, c, t)] = cell[: 3 * quarter]
                 short[(*place(1, j, t), pl.ds(h * quarter, quarter))] = cell[3 * quarter:]
         for kind, c in ((0, 2 * j), (0, 2 * j + 1), (1, j)):
-            exchange(kind, c, 0).start()
+            for copy in exchanges(kind, c, 0):
+                copy.start()
 
     for kind, c, s in ARRIVALS:
-        exchange(kind, c, s).wait_recv()
+        for copy in exchanges(kind, c, s):
+            copy.wait_recv()
         finish(kind, c, s)
     for j in range(pieces):
         cot_copy(j).wait_send()
     for g in range(groups):
         lhs_copy(g).wait_send()
     for kind, c, s in ARRIVALS:
-        exchange(kind, c, s).wait_send()
+        for copy in exchanges(kind, c, s):
+            copy.wait_send()
 
 
 def gradient(tokens, cotangent, devices):
@@ -180,17 +214,19 @@
             pltpu.VMEM((count, depth), bf16),
             pltpu.VMEM((2 * count, width), bf16),
             pltpu.VMEM((2, half, 2 * count), bf16),
-            *[pltpu.VMEM((chunks, *[2] * k, 3 * rows // 4, LANES), bf16) for k in (4, 3, 2, 1, 0)],
-            *[pltpu.VMEM((chunks // 2, *[2] * k, rows // 2, LANES), bf16) for k in (4, 3, 2, 1, 0)],
+            pltpu.VMEM((chunks, 16, 3 * rows // 4, LANES), bf16),
+            pltpu.VMEM((chunks, 15, 3 * rows // 4, LANES), bf16),
+            pltpu.VMEM((chunks // 2, 16, rows // 2, LANES), bf16),
+            pltpu.VMEM((chunks // 2, 15, rows // 2, LANES), bf16),
             pltpu.SemaphoreType.DMA((5,)),
             pltpu.SemaphoreType.DMA((width // WIDE,)),
             pltpu.SemaphoreType.DMA((width // WIDE,)),
             pltpu.SemaphoreType.DMA((4,)),
             pltpu.SemaphoreType.DMA((4,)),
-            pltpu.SemaphoreType.DMA((chunks, 4)),
-            pltpu.SemaphoreType.DMA((chunks, 4)),
-            pltpu.SemaphoreType.DMA((chunks // 2, 4)),
-            pltpu.SemaphoreType.DMA((chunks // 2, 4)),
+            pltpu.SemaphoreType.DMA((chunks, 6)),
+            pltpu.SemaphoreType.DMA((chunks, 6)),
+            pltpu.SemaphoreType.DMA((chunks // 2, 6)),
+            pltpu.SemaphoreType.DMA((chunks // 2, 6)),
         ],
         compiler_params=pltpu.CompilerParams(
             collective_id=0, has_side_effects=True, vmem_limit_bytes=62 * 1024 * 1024

time: 34.4 us -> 35.2 us (1.023)
  Pallas kernels: 31.5 us -> 32.3 us
    pallas_call x1, Pallas kernels: 31.5 us -> 32.3 us  [gradient(): pl.pallas_call(kernel, out_shape=jax.ShapeDtypeStruct((rows, width), jnp....]
where the time goes in v5:
time: 35.2 us; the launch traced here: 35 us
  Pallas kernels  32.3 us (92%)
  other arithmetic  2.02 us (6%)
  between operations  0.72 us (2%)
    pallas_call x1, Pallas kernels, gradient(): pl.pallas_call(kernel, out_shape=jax.ShapeDtypeStruct((rows, width), jnp....  32.3 us
    convert_element_type x1, other arithmetic, shards(): weight_next = outer_next.astype(jnp.bfloat16)  2.02 us

profile of v5, /device:TPU:0, one launch (start us, length us, event | category | flops | bytes accessed | tf_op | source)
XLA Modules:
  0.0 35.0 jit_solution(18388222811795250153)
XLA Ops:
  0.6 0.0 copy-start
  0.6 0.0 copy-start.1
  0.7 0.0 copy-start.2
  0.7 0.0 copy-start.3
  0.7 0.0 copy-start.4
  0.7 32.3 %shard_map.94 = f32[64,1024]{1,0:T(8,128)} custom-call(bf16[256,2048]{1,0:T(8,128)(2,1)} %bitcast.12, bf16[256,1024]{1,0:T(8,128)(2,1)} %bitcast.13), custom_call_target="tpu_custom_call" | custom-call | flops 1073741824 | bytes 1835008 | tf_op jit(solution)/shard_map/pallas_call | solution.py:208
  33.0 0.0 copy-done
  33.0 0.0 copy-done.1
  33.0 0.0 copy-done.2
  33.0 0.0 copy-done.3
  33.0 0.0 copy-done.4
  33.0 2.0 %fusion.7 = (bf16[64,1024]{1,0:T(8,128)(2,1)}, f32[64,1024]{1,0:T(8,128)}, f32[64,1024]{1,0:T(8,128)}) fusion(f32[64,1024]{1,0:T(8,128)S(1)} %copy-done, f32[64,1024]{1,0:T(8,128)S(1)} %copy-done.1, f32[64,1024]{1,0:T(8,128)} %shard_map.94, f32[1,64,1024]{2,1,0:T(8,128)S(1)} %copy-done.2, f32[1,64,1024]{2,1,0:T(8,128)S(1)} %copy-done.3, ...), kind=kLoop, calls=%fused_computation.11 | loop fusion | flops 1310720 | bytes 2228224 | tf_op jit(solution)/shard_map/convert_element_type | solution.py:257
Async XLA Ops:
  0.6 32.3 %copy-start = (f32[64,1024]{1,0:T(8,128)S(1)}, f32[64,1024]{1,0:T(8,128)}, u32[]{:S(2)}) copy-start(f32[64,1024]{1,0:T(8,128)} %param.12) | copy-start | bytes 786436
  0.6 32.3 %copy-start.1 = (f32[64,1024]{1,0:T(8,128)S(1)}, f32[64,1024]{1,0:T(8,128)}, u32[]{:S(2)}) copy-start(f32[64,1024]{1,0:T(8,128)} %param.13) | copy-start | bytes 786436
  0.7 32.3 %copy-start.2 = (f32[1,64,1024]{2,1,0:T(8,128)S(1)}, f32[1,64,1024]{2,1,0:T(8,128)}, u32[]{:S(2)}) copy-start(f32[1,64,1024]{2,1,0:T(8,128)} %param.11) | copy-start | bytes 786436
  0.7 32.3 %copy-start.3 = (f32[1,64,1024]{2,1,0:T(8,128)S(1)}, f32[1,64,1024]{2,1,0:T(8,128)}, u32[]{:S(2)}) copy-start(f32[1,64,1024]{2,1,0:T(8,128)} %param.10) | copy-start | bytes 786436
  0.7 32.3 %copy-start.4 = (f32[1,64,1024]{2,1,0:T(8,128)S(1)}, f32[1,64,1024]{2,1,0:T(8,128)}, u32[]{:S(2)}) copy-start(f32[1,64,1024]{2,1,0:T(8,128)} %param.9) | copy-start | bytes 786436

commit v6 on v5

--- a/solution.py
+++ b/solution.py
@@ -13,29 +13,30 @@
 MESH = pl.DeviceIdType.MESH
 
 TALL = (
-    ((4,), (1,), (2,), (3,)),
-    ((2,), (1,), (4,), (3,)),
-    ((3,), (1, 2), (4,)),
+    ((1,), (4,), (2,), (3,)),
     ((2,), (3,), (1,), (4,)),
-    ((1,), (2,), (3, 4)),
-    ((2,), (1,), (3, 4)),
-    ((1,), (2,), (3, 4)),
-    ((3,), (1, 2), (4,)),
+    ((3,), (2,), (4,), (1,)),
+    ((4,), (2,), (1,), (3,)),
+    ((1,), (2,), (4,), (3,)),
+    ((3,), (1,), (2,), (4,)),
+    ((1,), (2,), (3,), (4,)),
+    ((2,), (1,), (3,), (4,)),
 )
 SHORT = (
-    ((3,), (4,), (1,), (2,)),
-    ((1,), (2,), (3, 4)),
-    ((4,), (1,), (3,), (2,)),
-    ((1,), (2,), (3,), (4,)),
+    ((4,), (1,), (2,), (3,)),
+    ((2,), (1,), (3,), (4,)),
+    ((2,), (1,), (3,), (4,)),
+    ((1,), (2,), (4,), (3,)),
 )
 ARRIVALS = (
-    (1, 1, 0), (0, 1, 0), (1, 0, 0), (0, 3, 0), (1, 3, 0), (0, 5, 0),
-    (1, 1, 1), (0, 4, 0), (1, 2, 0), (0, 6, 0), (0, 0, 0), (0, 1, 1),
-    (1, 3, 1), (0, 2, 0), (0, 5, 1), (1, 1, 2), (0, 7, 0), (1, 2, 1),
-    (0, 4, 1), (1, 0, 1), (0, 6, 1), (0, 0, 1), (0, 3, 1), (1, 3, 2),
-    (0, 1, 2), (0, 2, 1), (0, 5, 2), (0, 7, 1), (1, 0, 2), (0, 0, 2),
-    (0, 3, 2), (1, 2, 2), (0, 4, 2), (1, 3, 3), (0, 6, 2), (0, 1, 3),
-    (1, 0, 3), (0, 2, 2), (0, 7, 2), (0, 0, 3), (1, 2, 3), (0, 3, 3),
+    (0, 0, 0), (0, 1, 0), (1, 0, 0), (0, 2, 0), (1, 1, 0), (0, 4, 0),
+    (1, 2, 0), (0, 6, 0), (0, 7, 0), (0, 3, 0), (0, 5, 0), (1, 3, 0),
+    (0, 2, 1), (1, 0, 1), (1, 1, 1), (0, 4, 1), (0, 0, 1), (0, 1, 1),
+    (1, 2, 1), (0, 6, 1), (1, 1, 2), (0, 2, 2), (0, 7, 1), (0, 3, 1),
+    (1, 2, 2), (0, 4, 2), (0, 5, 1), (1, 3, 1), (1, 0, 2), (0, 6, 2),
+    (0, 1, 2), (1, 1, 3), (0, 2, 3), (0, 0, 2), (0, 7, 2), (0, 3, 2),
+    (1, 2, 3), (0, 4, 3), (0, 5, 2), (1, 0, 3), (1, 3, 2), (0, 6, 3),
+    (0, 1, 3), (0, 0, 3), (0, 7, 3), (0, 3, 3), (1, 3, 3), (0, 5, 3),
 )
 
 
@@ -47,7 +48,7 @@
 
 def kernel(
     acts_hbm, cot_hbm, grad_ref,
-    acts, cot, lhs,
+    acts, cot, lhs, ahead,
     tall, tall_in, short, short_in,
     load_sem, cot_send, cot_recv, lhs_send, lhs_recv,
     tall_send, tall_recv, short_send, short_recv,
@@ -103,16 +104,22 @@
             lhs_send.at[g], lhs_recv.at[g],
         )
 
-    for t in range(tiles):
-        if t % (tiles // groups) == 0:
-            acts_copy(t // (tiles // groups)).wait()
-        turned = acts[:, t * LANES:(t + 1) * LANES].T
-        lhs[0, t * rows:(t + 1) * rows, :tokens] = turned[:rows]
-        lhs[1, t * rows:(t + 1) * rows, :tokens] = turned[rows:]
-    pl.semaphore_wait(barrier, 1 + len(partners))
-    cot_copy(0).start()
-    for g in range(groups):
+    def start_group(g):
         lhs_copy(g).start()
+        if g == 1:
+            cot_copy(0).start()
+
+    for g in range(groups):
+        acts_copy(g).wait()
+        for t in range(g * tiles // groups, (g + 1) * tiles // groups):
+            turned = acts[:, t * LANES:(t + 1) * LANES].T
+            lhs[0, t * rows:(t + 1) * rows, :tokens] = turned[:rows]
+            lhs[1, t * rows:(t + 1) * rows, :tokens] = turned[rows:]
+        if g == 1:
+            pl.semaphore_wait(barrier, 1 + len(partners))
+            start_group(0)
+        if g >= 1:
+            start_group(g)
     for j in range(1, pieces):
         cot_copy(j).start()
 
@@ -169,14 +176,25 @@
                 strip = slice((2 * c + h) * LANES, (2 * c + h + 1) * LANES)
                 grad_ref[3 * quarter:, strip] = total[h * quarter:(h + 1) * quarter]
 
+    def multiply(token_range, j):
+        return jnp.dot(
+            lhs[core, :, token_range], cot[token_range, j * WIDE:(j + 1) * WIDE],
+            preferred_element_type=jnp.float32,
+        )
+
     load_cot.wait()
+    early = ahead.shape[0]
+    for j in range(early):
+        ahead[j] = multiply(slice(0, tokens), j)
     for g in range(groups):
         lhs_copy(g).wait_recv()
     for j in range(pieces):
         cot_copy(j).wait_recv()
-        product = jnp.dot(
-            lhs[core], cot[:, j * WIDE:(j + 1) * WIDE], preferred_element_type=jnp.float32
-        ).astype(jnp.bfloat16)
+        if j < early:
+            product = ahead[j] + multiply(slice(tokens, 2 * tokens), j)
+        else:
+            product = multiply(slice(0, 2 * tokens), j)
+        product = product.astype(jnp.bfloat16)
         for t in range(tiles):
             for h in range(2):
                 c = 2 * j + h
@@ -214,6 +232,7 @@
             pltpu.VMEM((count, depth), bf16),
             pltpu.VMEM((2 * count, width), bf16),
             pltpu.VMEM((2, half, 2 * count), bf16),
+            pltpu.VMEM((2, half, WIDE), jnp.float32),
             pltpu.VMEM((chunks, 16, 3 * rows // 4, LANES), bf16),
             pltpu.VMEM((chunks, 15, 3 * rows // 4, LANES), bf16),
             pltpu.VMEM((chunks // 2, 16, rows // 2, LANES), bf16),

time: 35.2 us -> 34.2 us (0.972)
  Pallas kernels: 32.3 us -> 31.3 us
    pallas_call x1, Pallas kernels: 32.3 us -> 31.3 us  [gradient(): pl.pallas_call(kernel, out_shape=jax.ShapeDtypeStruct((rows, width), jnp....]
where the time goes in v6:
time: 34.2 us; the launch traced here: 34.1 us
  Pallas kernels  31.3 us (92%)
  other arithmetic  2.02 us (6%)
  between operations  0.72 us (2%)
    pallas_call x1, Pallas kernels, gradient(): pl.pallas_call(kernel, out_shape=jax.ShapeDtypeStruct((rows, width), jnp....  31.3 us
    convert_element_type x1, other arithmetic, shards(): weight_next = outer_next.astype(jnp.bfloat16)  2.02 us

profile of v6, /device:TPU:0, one launch (start us, length us, event | category | flops | bytes accessed | tf_op | source)
XLA Modules:
  0.0 34.1 jit_solution(10892577477440453883)
XLA Ops:
  0.6 0.0 copy-start
  0.6 0.0 copy-start.1
  0.7 0.0 copy-start.2
  0.7 0.0 copy-start.3
  0.7 0.0 copy-start.4
  0.7 31.3 %shard_map.94 = f32[64,1024]{1,0:T(8,128)} custom-call(bf16[256,2048]{1,0:T(8,128)(2,1)} %bitcast.12, bf16[256,1024]{1,0:T(8,128)(2,1)} %bitcast.13), custom_call_target="tpu_custom_call" | custom-call | flops 1073741824 | bytes 1835008 | tf_op jit(solution)/shard_map/pallas_call | solution.py:226
  32.0 0.0 copy-done
  32.0 0.0 copy-done.1
  32.0 0.0 copy-done.2
  32.0 0.0 copy-done.3
  32.0 0.0 copy-done.4
  32.0 2.0 %fusion.7 = (bf16[64,1024]{1,0:T(8,128)(2,1)}, f32[64,1024]{1,0:T(8,128)}, f32[64,1024]{1,0:T(8,128)}) fusion(f32[64,1024]{1,0:T(8,128)S(1)} %copy-done, f32[64,1024]{1,0:T(8,128)S(1)} %copy-done.1, f32[64,1024]{1,0:T(8,128)} %shard_map.94, f32[1,64,1024]{2,1,0:T(8,128)S(1)} %copy-done.2, f32[1,64,1024]{2,1,0:T(8,128)S(1)} %copy-done.3, ...), kind=kLoop, calls=%fused_computation.11 | loop fusion | flops 1310720 | bytes 2228224 | tf_op jit(solution)/shard_map/convert_element_type | solution.py:276
Async XLA Ops:
  0.6 31.4 %copy-start = (f32[64,1024]{1,0:T(8,128)S(1)}, f32[64,1024]{1,0:T(8,128)}, u32[]{:S(2)}) copy-start(f32[64,1024]{1,0:T(8,128)} %param.12) | copy-start | bytes 786436
  0.6 31.4 %copy-start.1 = (f32[64,1024]{1,0:T(8,128)S(1)}, f32[64,1024]{1,0:T(8,128)}, u32[]{:S(2)}) copy-start(f32[64,1024]{1,0:T(8,128)} %param.13) | copy-start | bytes 786436
  0.7 31.4 %copy-start.2 = (f32[1,64,1024]{2,1,0:T(8,128)S(1)}, f32[1,64,1024]{2,1,0:T(8,128)}, u32[]{:S(2)}) copy-start(f32[1,64,1024]{2,1,0:T(8,128)} %param.11) | copy-start | bytes 786436
  0.7 31.4 %copy-start.3 = (f32[1,64,1024]{2,1,0:T(8,128)S(1)}, f32[1,64,1024]{2,1,0:T(8,128)}, u32[]{:S(2)}) copy-start(f32[1,64,1024]{2,1,0:T(8,128)} %param.10) | copy-start | bytes 786436
  0.7 31.4 %copy-start.4 = (f32[1,64,1024]{2,1,0:T(8,128)S(1)}, f32[1,64,1024]{2,1,0:T(8,128)}, u32[]{:S(2)}) copy-start(f32[1,64,1024]{2,1,0:T(8,128)} %param.9) | copy-start | bytes 786436

commit v7 on v0

v7 whole, which is shorter than its diff:
```python
import functools

import jax
import jax.numpy as jnp
from jax import lax
from jax.experimental import pallas as pl
from jax.experimental.pallas import tpu as pltpu
from jax.sharding import PartitionSpec as P

INNER_STEP = 500
LANES = 128
WIDE = 2 * LANES
MESH = pl.DeviceIdType.MESH

ORDERS = ((1, 2, 3, 4), (2, 1, 3, 4), (3, 1, 2, 4))


def kernel(
    acts_hbm, cot_hbm, grad_ref,
    acts, cot, lhs, left, right, low, left_in, right_in, low_in,
    load_sem, cot_send, cot_recv, lhs_send, lhs_recv, send_sem, recv_sem,
):
    me = lax.axis_index("fsdp")
    bit = [lax.rem(me // (1 << b), 2) for b in range(5)]
    peer = [{"fsdp": me + (1 - 2 * bit[b]) * (1 << b)} for b in range(5)]
    core = bit[0]
    tokens, width = acts.shape[0], cot.shape[1]
    rows, tiles = grad_ref.shape[0], acts.shape[1] // LANES
    groups = 4
    group_rows, group_tiles = lhs.shape[1] // groups, tiles // groups
    pieces = width // WIDE
    quarter = rows // 4
    parts, incoming = (left, right, low), (left_in, right_in, low_in)
    span = acts.shape[1] // groups

    def each(count, body):
        def run(i, carry):
            body(i)
            return carry

        lax.fori_loop(0, count, run, 0)

    def lanes(i, size):
        return pl.ds(pl.multiple_of(i * size, size), size)

    def acts_copy(g):
        cut = lanes(g, span)
        return pltpu.make_async_copy(acts_hbm.at[:, cut], acts.at[:, cut], load_sem.at[g])

    each(groups, lambda g: acts_copy(g).start())
    load_cot = pltpu.make_async_copy(cot_hbm, cot.at[:tokens], load_sem.at[groups])
    load_cot.start()
    barrier = pltpu.get_barrier_semaphore()
    for b in range(5):
        pl.semaphore_signal(barrier, inc=1, device_id=peer[b], device_id_type=MESH)

    def to_core(src, dst, send, recv):
        return pltpu.make_async_remote_copy(
            src_ref=src, dst_ref=dst, send_sem=send, recv_sem=recv,
            device_id=peer[0], device_id_type=MESH,
        )

    def cot_copy(j):
        cut = lanes(j, WIDE)
        return to_core(cot_hbm.at[:, cut], cot.at[tokens:, cut], cot_send.at[j], cot_recv.at[j])

    def lhs_copy(g):
        cut = lanes(g, group_rows)
        return to_core(
            lhs.at[1 - core, cut, :tokens], lhs.at[1 - core, cut, tokens:],
            lhs_send.at[g], lhs_recv.at[g],
        )

    def turn_group(g):
        acts_copy(g).wait()

        def turn(k):
            t = g * group_tiles + k
            turned = acts[:, lanes(t, LANES)].T
            lhs[0, lanes(t, rows), :tokens] = turned[:rows]
            lhs[1, lanes(t, rows), :tokens] = turned[rows:]

        each(group_tiles, turn)

    def turn_and_send(g):
        turn_group(g)
        lhs_copy(g).start()

    turn_group(0)
    pl.semaphore_wait(barrier, 5)
    lhs_copy(0).start()
    cot_copy(0).start()
    each(groups - 1, lambda g: turn_and_send(g + 1))
    each(pieces - 1, lambda j: cot_copy(j + 1).start())

    def exchange(kind, j, s):
        order, start = ORDERS[kind], 0
        for i in range(s):
            start += bit[order[i]] * (8 >> i)
        start += (1 - bit[order[s]]) * (8 >> s)
        return pltpu.make_async_remote_copy(
            src_ref=parts[kind].at[j, pl.ds(start, 8 >> s)],
            dst_ref=incoming[kind].at[j, pl.ds(16 - (16 >> s), 8 >> s)],
            send_sem=send_sem.at[kind, j, s],
            recv_sem=recv_sem.at[kind, j, s],
            device_id=peer[order[s]],
            device_id_type=MESH,
        )

    def place(kind, t):
        return sum((t >> (b - 1) & 1) * (8 >> i) for i, b in enumerate(ORDERS[kind]))

    def multiply(j):
        cot_copy(j).wait_recv()
        product = jnp.dot(
            lhs[core], cot[:, lanes(j, WIDE)], preferred_element_type=jnp.float32
        ).astype(jnp.bfloat16)
        for t in range(tiles):
            cell = product[t * rows:(t + 1) * rows]
            left[j, place(0, t)] = cell[: 3 * quarter, :LANES]
            right[j, place(1, t)] = cell[: 3 * quarter, LANES:]
            low[j, place(2, t), :quarter] = cell[3 * quarter:, :LANES]
            low[j, place(2, t), quarter:] = cell[3 * quarter:, LANES:]
        for kind in range(3):
            exchange(kind, j, 0).start()

    load_cot.wait()
    each(groups, lambda g: lhs_copy(g).wait_recv())
    each(pieces, multiply)

    def finish(kind, j, s):
        exchange(kind, j, s).wait_recv()
        start, count = sum(bit[b] * (8 >> i) for i, b in enumerate(ORDERS[kind][: s + 1])), 8 >> s
        ours = parts[kind][j, pl.ds(start, count)]
        theirs = incoming[kind][j, 16 - 2 * count:16 - count]
        if s < 3:
            parts[kind][j, pl.ds(start, count)] = ours + theirs
            exchange(kind, j, s + 1).start()
            return
        total = ours[0].astype(jnp.float32) + theirs[0].astype(jnp.float32)
        if kind < 2:
            grad_ref[: 3 * quarter, lanes(2 * j + kind, LANES)] = total
        else:
            grad_ref[3 * quarter:, lanes(2 * j, LANES)] = total[:quarter]
            grad_ref[3 * quarter:, lanes(2 * j + 1, LANES)] = total[quarter:]

    def finish_piece(s, j):
        for kind in range(3):
            finish(kind, j, s)

    def drain(s, j):
        for kind in range(3):
            exchange(kind, j, s).wait_send()

    for s in range(4):
        each(pieces, functools.partial(finish_piece, s))
    each(pieces, lambda j: cot_copy(j).wait_send())
    each(groups, lambda g: lhs_copy(g).wait_send())
    for s in range(4):
        each(pieces, functools.partial(drain, s))


def gradient(tokens, cotangent, devices):
    count, depth = tokens.shape
    width = cotangent.shape[1]
    rows, half, pieces = depth // devices, depth // 2, width // WIDE
    bf16 = jnp.bfloat16
    return pl.pallas_call(
        kernel,
        out_shape=jax.ShapeDtypeStruct((rows, width), jnp.float32),
        in_specs=[pl.BlockSpec(memory_space=pltpu.HBM)] * 2,
        out_specs=pl.BlockSpec(memory_space=pltpu.VMEM),
        scratch_shapes=[
            pltpu.VMEM((count, depth), bf16),
            pltpu.VMEM((2 * count, width), bf16),
            pltpu.VMEM((2, half, 2 * count), bf16),
            pltpu.VMEM((pieces, 16, 3 * rows // 4, LANES), bf16),
            pltpu.VMEM((pieces, 16, 3 * rows // 4, LANES), bf16),
            pltpu.VMEM((pieces, 16, rows // 2, LANES), bf16),
            pltpu.VMEM((pieces, 15, 3 * rows // 4, LANES), bf16),
            pltpu.VMEM((pieces, 15, 3 * rows // 4, LANES), bf16),
            pltpu.VMEM((pieces, 15, rows // 2, LANES), bf16),
            pltpu.SemaphoreType.DMA((5,)),
            pltpu.SemaphoreType.DMA((pieces,)),
            pltpu.SemaphoreType.DMA((pieces,)),
            pltpu.SemaphoreType.DMA((4,)),
            pltpu.SemaphoreType.DMA((4,)),
            pltpu.SemaphoreType.DMA((3, pieces, 4)),
            pltpu.SemaphoreType.DMA((3, pieces, 4)),
        ],
        compiler_params=pltpu.CompilerParams(
            collective_id=0, has_side_effects=True, vmem_limit_bytes=62 * 1024 * 1024
        ),
        cost_estimate=pl.CostEstimate(
            flops=2 * count * depth * width,
            bytes_accessed=2 * count * (depth + width) + 4 * rows * width,
            transcendentals=0,
        ),
    )(tokens, cotangent)


def shards(devices, acts, grad_out, inner_weight, first_moment, second_moment, outer_weight, outer_momentum):
    grad = gradient(acts[0], grad_out[0], devices)
    first = 0.9 * first_moment[0] + 0.1 * grad
    second = 0.95 * second_moment[0] + 0.05 * grad * grad
    first_hat = first / (1.0 - 0.9**INNER_STEP)
    second_hat = second / (1.0 - 0.95**INNER_STEP)
    inner_new = inner_weight[0] * (1.0 - 0.0004 * 0.1) - 0.0004 * first_hat / (
        jnp.sqrt(second_hat) + 1e-08
    )
    replicas = lax.axis_size("rep")
    if replicas > 1:
        inner_new = lax.psum_scatter(inner_new, "rep", scatter_dimension=0, tiled=True) / replicas
    pseudo = outer_weight - inner_new
    momentum_next = 0.9 * outer_momentum + pseudo
    outer_next = outer_weight - 0.7 * (pseudo + 0.9 * momentum_next)
    weight_next = outer_next.astype(jnp.bfloat16)
    if replicas > 1:
        weight_next = lax.all_gather(weight_next, "rep", axis=0, tiled=True)
    return (outer_next, momentum_next, weight_next)


def solution(mesh):
    placed = (
        P("rep", "fsdp", None),
        P("rep", "fsdp", None),
        P("rep", "fsdp", None),
        P("rep", "fsdp", None),
        P("rep", "fsdp", None),
        P(("fsdp", "rep"), None),
        P(("fsdp", "rep"), None),
    )
    return jax.shard_map(
        functools.partial(shards, mesh.shape["fsdp"]),
        mesh=mesh,
        in_specs=placed,
        out_specs=(P(("fsdp", "rep"), None), P(("fsdp", "rep"), None), P("fsdp", None)),
        check_vma=False,
    )
```

time: 165 us -> 37.3 us (0.23)
  waiting for transfers between devices: 144 us -> 0 us
  Pallas kernels: 0 us -> 34.4 us
  between operations: 14.1 us -> 0.72 us
  matrix products: 4.27 us -> 0 us
    reduce_scatter x1 -> x0, waiting for transfers between devices: 144 us -> none  [shards(): lax.psum_scatter(lax.dot_general(tokens, cotangent, (((0,), (0,)), ((), (...]
    pallas_call x0 -> x1, Pallas kernels: none -> 34.4 us  [gradient(): pl.pallas_call(kernel, out_shape=jax.ShapeDtypeStruct((rows, width), jnp....]
    dot_general x1 -> x0, matrix products: 4.27 us -> none  [shards(): lax.dot_general(tokens, cotangent, (((0,), (0,)), ((), ())), preferred_el...]
  transfers between devices with their start and end apart: 1 -> 0, of which waited for: 1 -> 0; matrix products, arithmetic and copies ran while one was open for 0% -> 0% of each run, Pallas kernels for 0% -> 0%
where the time goes in v7:
time: 37.3 us; the launch traced here: 37.2 us
  Pallas kernels  34.4 us (92%)
  other arithmetic  2.02 us (5%)
  between operations  0.72 us (2%)
    pallas_call x1, Pallas kernels, gradient(): pl.pallas_call(kernel, out_shape=jax.ShapeDtypeStruct((rows, width), jnp....  34.4 us
    convert_element_type x1, other arithmetic, shards(): weight_next = outer_next.astype(jnp.bfloat16)  2.02 us

profile of v7, /device:TPU:0, one launch (start us, length us, event | category | flops | bytes accessed | tf_op | source)
XLA Modules:
  0.0 37.2 jit_solution(3561712625722662904)
XLA Ops:
  0.6 0.0 copy-start
  0.6 0.0 copy-start.1
  0.7 0.0 copy-start.2
  0.7 0.0 copy-start.3
  0.7 0.0 copy-start.4
  0.7 34.4 %shard_map.94 = f32[64,1024]{1,0:T(8,128)} custom-call(bf16[256,2048]{1,0:T(8,128)(2,1)} %bitcast.12, bf16[256,1024]{1,0:T(8,128)(2,1)} %bitcast.13), custom_call_target="tpu_custom_call" | custom-call | flops 1073741824 | bytes 1835008 | tf_op jit(solution)/shard_map/pallas_call | solution.py:168
  35.1 0.0 copy-done
  35.1 0.0 copy-done.1
  35.1 0.0 copy-done.2
  35.1 0.0 copy-done.3
  35.1 0.0 copy-done.4
  35.1 2.0 %fusion.7 = (bf16[64,1024]{1,0:T(8,128)(2,1)}, f32[64,1024]{1,0:T(8,128)}, f32[64,1024]{1,0:T(8,128)}) fusion(f32[64,1024]{1,0:T(8,128)S(1)} %copy-done, f32[64,1024]{1,0:T(8,128)S(1)} %copy-done.1, f32[64,1024]{1,0:T(8,128)} %shard_map.94, f32[1,64,1024]{2,1,0:T(8,128)S(1)} %copy-done.2, f32[1,64,1024]{2,1,0:T(8,128)S(1)} %copy-done.3, ...), kind=kLoop, calls=%fused_computation.11 | loop fusion | flops 1310720 | bytes 2228224 | tf_op jit(solution)/shard_map/convert_element_type | solution.py:217
Async XLA Ops:
  0.6 34.4 %copy-start = (f32[64,1024]{1,0:T(8,128)S(1)}, f32[64,1024]{1,0:T(8,128)}, u32[]{:S(2)}) copy-start(f32[64,1024]{1,0:T(8,128)} %param.12) | copy-start | bytes 786436
  0.6 34.4 %copy-start.1 = (f32[64,1024]{1,0:T(8,128)S(1)}, f32[64,1024]{1,0:T(8,128)}, u32[]{:S(2)}) copy-start(f32[64,1024]{1,0:T(8,128)} %param.13) | copy-start | bytes 786436
  0.7 34.4 %copy-start.2 = (f32[1,64,1024]{2,1,0:T(8,128)S(1)}, f32[1,64,1024]{2,1,0:T(8,128)}, u32[]{:S(2)}) copy-start(f32[1,64,1024]{2,1,0:T(8,128)} %param.11) | copy-start | bytes 786436
  0.7 34.4 %copy-start.3 = (f32[1,64,1024]{2,1,0:T(8,128)S(1)}, f32[1,64,1024]{2,1,0:T(8,128)}, u32[]{:S(2)}) copy-start(f32[1,64,1024]{2,1,0:T(8,128)} %param.10) | copy-start | bytes 786436
  0.7 34.4 %copy-start.4 = (f32[1,64,1024]{2,1,0:T(8,128)S(1)}, f32[1,64,1024]{2,1,0:T(8,128)}, u32[]{:S(2)}) copy-start(f32[1,64,1024]{2,1,0:T(8,128)} %param.9) | copy-start | bytes 786436

commit v8 on v6

--- a/solution.py
+++ b/solution.py
@@ -48,7 +48,7 @@
 
 def kernel(
     acts_hbm, cot_hbm, grad_ref,
-    acts, cot, lhs, ahead,
+    acts, cot, lhs,
     tall, tall_in, short, short_in,
     load_sem, cot_send, cot_recv, lhs_send, lhs_recv,
     tall_send, tall_recv, short_send, short_recv,
@@ -95,13 +95,13 @@
 
     def cot_copy(j):
         cut = pl.ds(j * WIDE, WIDE)
-        return to_core(cot_hbm.at[:, cut], cot.at[tokens:, cut], cot_send.at[j], cot_recv.at[j])
+        return to_core(cot_hbm.at[:, cut], cot.at[tokens:, cut], cot_send, cot_recv.at[j])
 
     def lhs_copy(g):
         cut = pl.ds(g * group_rows, group_rows)
         return to_core(
             lhs.at[1 - core, cut, :tokens], lhs.at[1 - core, cut, tokens:],
-            lhs_send.at[g], lhs_recv.at[g],
+            lhs_send, lhs_recv,
         )
 
     def start_group(g):
@@ -136,7 +136,7 @@
             copies.append(pltpu.make_async_remote_copy(
                 src_ref=part.at[c, pl.ds(start, count)],
                 dst_ref=incoming.at[c, pl.ds(slot, count)],
-                send_sem=send.at[c, sem],
+                send_sem=send,
                 recv_sem=recv.at[c, sem],
                 device_id=device(flipped),
                 device_id_type=MESH,
@@ -176,24 +176,14 @@
                 strip = slice((2 * c + h) * LANES, (2 * c + h + 1) * LANES)
                 grad_ref[3 * quarter:, strip] = total[h * quarter:(h + 1) * quarter]
 
-    def multiply(token_range, j):
-        return jnp.dot(
-            lhs[core, :, token_range], cot[token_range, j * WIDE:(j + 1) * WIDE],
-            preferred_element_type=jnp.float32,
-        )
-
     load_cot.wait()
-    early = ahead.shape[0]
-    for j in range(early):
-        ahead[j] = multiply(slice(0, tokens), j)
-    for g in range(groups):
-        lhs_copy(g).wait_recv()
+    all_rows = lhs.at[1 - core, :, :tokens]
+    to_core(all_rows, lhs.at[1 - core, :, tokens:], lhs_send, lhs_recv).wait_recv()
     for j in range(pieces):
         cot_copy(j).wait_recv()
-        if j < early:
-            product = ahead[j] + multiply(slice(tokens, 2 * tokens), j)
-        else:
-            product = multiply(slice(0, 2 * tokens), j)
+        product = jnp.dot(
+            lhs[core], cot[:, j * WIDE:(j + 1) * WIDE], preferred_element_type=jnp.float32
+        )
         product = product.astype(jnp.bfloat16)
         for t in range(tiles):
             for h in range(2):
@@ -209,13 +199,10 @@
         for copy in exchanges(kind, c, s):
             copy.wait_recv()
         finish(kind, c, s)
-    for j in range(pieces):
-        cot_copy(j).wait_send()
-    for g in range(groups):
-        lhs_copy(g).wait_send()
-    for kind, c, s in ARRIVALS:
-        for copy in exchanges(kind, c, s):
-            copy.wait_send()
+    to_core(cot_hbm, cot.at[tokens:], cot_send, cot_recv.at[0]).wait_send()
+    to_core(all_rows, lhs.at[1 - core, :, tokens:], lhs_send, lhs_recv).wait_send()
+    to_core(tall_in, tall_in, tall_send, tall_recv.at[0, 0]).wait_send()
+    to_core(short_in, short_in, short_send, short_recv.at[0, 0]).wait_send()
 
 
 def gradient(tokens, cotangent, devices):
@@ -232,20 +219,19 @@
             pltpu.VMEM((count, depth), bf16),
             pltpu.VMEM((2 * count, width), bf16),
             pltpu.VMEM((2, half, 2 * count), bf16),
-            pltpu.VMEM((2, half, WIDE), jnp.float32),
             pltpu.VMEM((chunks, 16, 3 * rows // 4, LANES), bf16),
             pltpu.VMEM((chunks, 15, 3 * rows // 4, LANES), bf16),
             pltpu.VMEM((chunks // 2, 16, rows // 2, LANES), bf16),
             pltpu.VMEM((chunks // 2, 15, rows // 2, LANES), bf16),
             pltpu.SemaphoreType.DMA((5,)),
+            pltpu.SemaphoreType.DMA,
             pltpu.SemaphoreType.DMA((width // WIDE,)),
-            pltpu.SemaphoreType.DMA((width // WIDE,)),
-            pltpu.SemaphoreType.DMA((4,)),
-            pltpu.SemaphoreType.DMA((4,)),
-            pltpu.SemaphoreType.DMA((chunks, 6)),
-            pltpu.SemaphoreType.DMA((chunks, 6)),
-            pltpu.SemaphoreType.DMA((chunks // 2, 6)),
-            pltpu.SemaphoreType.DMA((chunks // 2, 6)),
+            pltpu.SemaphoreType.DMA,
+            pltpu.SemaphoreType.DMA,
+            pltpu.SemaphoreType.DMA,
+            pltpu.SemaphoreType.DMA((chunks, 4)),
+            pltpu.SemaphoreType.DMA,
+            pltpu.SemaphoreType.DMA((chunks // 2, 4)),
         ],
         compiler_params=pltpu.CompilerParams(
             collective_id=0, has_side_effects=True, vmem_limit_bytes=62 * 1024 * 1024

time: 34.2 us -> 33.5 us (0.980)
  Pallas kernels: 31.3 us -> 30.6 us
    pallas_call x1, Pallas kernels: 31.3 us -> 30.6 us  [gradient(): pl.pallas_call(kernel, out_shape=jax.ShapeDtypeStruct((rows, width), jnp....]
where the time goes in v8:
time: 33.5 us; the launch traced here: 33.3 us
  Pallas kernels  30.6 us (91%)
  other arithmetic  2.02 us (6%)
  between operations  0.72 us (2%)
    pallas_call x1, Pallas kernels, gradient(): pl.pallas_call(kernel, out_shape=jax.ShapeDtypeStruct((rows, width), jnp....  30.6 us
    convert_element_type x1, other arithmetic, shards(): weight_next = outer_next.astype(jnp.bfloat16)  2.02 us

profile of v8, /device:TPU:0, one launch (start us, length us, event | category | flops | bytes accessed | tf_op | source)
XLA Modules:
  0.0 33.3 jit_solution(10824173989097568861)
XLA Ops:
  0.6 0.0 copy-start
  0.6 0.0 copy-start.1
  0.7 0.0 copy-start.2
  0.7 0.0 copy-start.3
  0.7 0.0 copy-start.4
  0.7 30.6 %shard_map.94 = f32[64,1024]{1,0:T(8,128)} custom-call(bf16[256,2048]{1,0:T(8,128)(2,1)} %bitcast.12, bf16[256,1024]{1,0:T(8,128)(2,1)} %bitcast.13), custom_call_target="tpu_custom_call" | custom-call | flops 1073741824 | bytes 1835008 | tf_op jit(solution)/shard_map/pallas_call | solution.py:213
  31.3 0.0 copy-done
  31.3 0.0 copy-done.1
  31.3 0.0 copy-done.2
  31.3 0.0 copy-done.3
  31.3 0.0 copy-done.4
  31.3 2.0 %fusion.7 = (bf16[64,1024]{1,0:T(8,128)(2,1)}, f32[64,1024]{1,0:T(8,128)}, f32[64,1024]{1,0:T(8,128)}) fusion(f32[64,1024]{1,0:T(8,128)S(1)} %copy-done, f32[64,1024]{1,0:T(8,128)S(1)} %copy-done.1, f32[64,1024]{1,0:T(8,128)} %shard_map.94, f32[1,64,1024]{2,1,0:T(8,128)S(1)} %copy-done.2, f32[1,64,1024]{2,1,0:T(8,128)S(1)} %copy-done.3, ...), kind=kLoop, calls=%fused_computation.11 | loop fusion | flops 1310720 | bytes 2228224 | tf_op jit(solution)/shard_map/convert_element_type | solution.py:262
Async XLA Ops:
  0.6 30.6 %copy-start = (f32[64,1024]{1,0:T(8,128)S(1)}, f32[64,1024]{1,0:T(8,128)}, u32[]{:S(2)}) copy-start(f32[64,1024]{1,0:T(8,128)} %param.12) | copy-start | bytes 786436
  0.6 30.6 %copy-start.1 = (f32[64,1024]{1,0:T(8,128)S(1)}, f32[64,1024]{1,0:T(8,128)}, u32[]{:S(2)}) copy-start(f32[64,1024]{1,0:T(8,128)} %param.13) | copy-start | bytes 786436
  0.7 30.6 %copy-start.2 = (f32[1,64,1024]{2,1,0:T(8,128)S(1)}, f32[1,64,1024]{2,1,0:T(8,128)}, u32[]{:S(2)}) copy-start(f32[1,64,1024]{2,1,0:T(8,128)} %param.11) | copy-start | bytes 786436
  0.7 30.6 %copy-start.3 = (f32[1,64,1024]{2,1,0:T(8,128)S(1)}, f32[1,64,1024]{2,1,0:T(8,128)}, u32[]{:S(2)}) copy-start(f32[1,64,1024]{2,1,0:T(8,128)} %param.10) | copy-start | bytes 786436
  0.7 30.6 %copy-start.4 = (f32[1,64,1024]{2,1,0:T(8,128)S(1)}, f32[1,64,1024]{2,1,0:T(8,128)}, u32[]{:S(2)}) copy-start(f32[1,64,1024]{2,1,0:T(8,128)} %param.9) | copy-start | bytes 786436

commit v9 on v8

--- a/solution.py
+++ b/solution.py
@@ -234,7 +234,7 @@
             pltpu.SemaphoreType.DMA((chunks // 2, 4)),
         ],
         compiler_params=pltpu.CompilerParams(
-            collective_id=0, has_side_effects=True, vmem_limit_bytes=62 * 1024 * 1024
+            collective_id=0, has_side_effects=True, vmem_limit_bytes=54720 * 1024
         ),
         cost_estimate=pl.CostEstimate(
             flops=2 * count * depth * width,

time: 33.5 us -> 31.8 us (0.949)
  other arithmetic: 2.02 us -> 1.07 us
  Pallas kernels: 30.6 us -> 29.9 us
    convert_element_type x1, other arithmetic: 2.02 us -> 1.07 us  [shards(): weight_next = outer_next.astype(jnp.bfloat16)]
    pallas_call x1, Pallas kernels: 30.6 us -> 29.9 us  [gradient(): pl.pallas_call(kernel, out_shape=jax.ShapeDtypeStruct((rows, width), jnp....]
where the time goes in v9:
time: 31.8 us; the launch traced here: 31.7 us
  Pallas kernels  29.9 us (94%)
  other arithmetic  1.07 us (3%)
  between operations  0.72 us (2%)
    pallas_call x1, Pallas kernels, gradient(): pl.pallas_call(kernel, out_shape=jax.ShapeDtypeStruct((rows, width), jnp....  29.9 us
    convert_element_type x1, other arithmetic, shards(): weight_next = outer_next.astype(jnp.bfloat16)  1.07 us

profile of v9, /device:TPU:0, one launch (start us, length us, event | category | flops | bytes accessed | tf_op | source)
XLA Modules:
  0.0 31.7 jit_solution(4713861344197523775)
XLA Ops:
  0.6 0.0 copy-start
  0.6 0.0 copy-start.1
  0.7 0.0 copy-start.2
  0.7 0.0 copy-start.3
  0.7 0.0 copy-start.4
  0.7 29.9 %shard_map.94 = f32[64,1024]{1,0:T(8,128)S(1)} custom-call(bf16[256,2048]{1,0:T(8,128)(2,1)} %bitcast.12, bf16[256,1024]{1,0:T(8,128)(2,1)} %bitcast.13), custom_call_target="tpu_custom_call" | custom-call | flops 1073741824 | bytes 1835008 | tf_op jit(solution)/shard_map/pallas_call | solution.py:213
  30.6 0.0 copy-done
  30.6 0.0 copy-done.1
  30.6 0.0 copy-done.2
  30.6 0.0 copy-done.3
  30.6 0.0 copy-done.4
  30.6 1.1 %fusion.7 = (bf16[64,1024]{1,0:T(8,128)(2,1)}, f32[64,1024]{1,0:T(8,128)}, f32[64,1024]{1,0:T(8,128)}) fusion(f32[64,1024]{1,0:T(8,128)S(1)} %copy-done, f32[64,1024]{1,0:T(8,128)S(1)} %copy-done.1, f32[64,1024]{1,0:T(8,128)S(1)} %shard_map.94, f32[1,64,1024]{2,1,0:T(8,128)S(1)} %copy-done.2, f32[1,64,1024]{2,1,0:T(8,128)S(1)} %copy-done.3, ...), kind=kLoop, calls=%fused_computation.11 | loop fusion | flops 1310720 | bytes 2228224 | tf_op jit(solution)/shard_map/convert_element_type | solution.py:262
Async XLA Ops:
  0.6 29.9 %copy-start = (f32[64,1024]{1,0:T(8,128)S(1)}, f32[64,1024]{1,0:T(8,128)}, u32[]{:S(2)}) copy-start(f32[64,1024]{1,0:T(8,128)} %param.12) | copy-start | bytes 786436
  0.6 29.9 %copy-start.1 = (f32[64,1024]{1,0:T(8,128)S(1)}, f32[64,1024]{1,0:T(8,128)}, u32[]{:S(2)}) copy-start(f32[64,1024]{1,0:T(8,128)} %param.13) | copy-start | bytes 786436
  0.7 29.9 %copy-start.2 = (f32[1,64,1024]{2,1,0:T(8,128)S(1)}, f32[1,64,1024]{2,1,0:T(8,128)}, u32[]{:S(2)}) copy-start(f32[1,64,1024]{2,1,0:T(8,128)} %param.11) | copy-start | bytes 786436
  0.7 29.9 %copy-start.3 = (f32[1,64,1024]{2,1,0:T(8,128)S(1)}, f32[1,64,1024]{2,1,0:T(8,128)}, u32[]{:S(2)}) copy-start(f32[1,64,1024]{2,1,0:T(8,128)} %param.10) | copy-start | bytes 786436
  0.7 29.9 %copy-start.4 = (f32[1,64,1024]{2,1,0:T(8,128)S(1)}, f32[1,64,1024]{2,1,0:T(8,128)}, u32[]{:S(2)}) copy-start(f32[1,64,1024]{2,1,0:T(8,128)} %param.9) | copy-start | bytes 786436
